TPU v7x, 32 devices: a whole 2x2x4 slice. The times are simulated.
32 devices in a mesh: leaf: 8 (over z, x), rows: 4 (over y, core).
Axes of the slice: x: 2, y: 2, z: 4, core: 2. Of those that a mesh axis runs over, the one named last changes fastest.
Arguments:
- child_front_entries: float32 [8, 4, 4, 128, 2048], P('leaf', None, 'rows'), may hold values from 0 to 2, as said below
- parent_fronts: float32 [8, 4, 4, 128, 2048], P('leaf', None, 'rows'), may hold values from 0 to 2, as said below
- parent_of: int32 [8], replicated, may hold values from 0 to 3, never falling along the last dimension, each value on 1 to 4 neighbouring positions
- positions: int32 [8, 8], P('leaf'), may hold values from 0 to 15, as said below
Outputs:
- child_factor: float32 [8, 4, 4, 128, 1024], P('leaf', None, 'rows')
- parent_factor: float32 [8, 4, 4, 128, 1024], P('leaf', None, 'rows')
- parent_contribution_block: float32 [8, 2, 4, 128, 1024], P('leaf', None, 'rows')
Inputs may be any that keep to these rules, and one draw needn't show every extreme that they name: `parent_of`: children of one parent stand at consecutive indices, at most 4 of them, and some parent has exactly 4; every parent has a child. `positions`: each row lists 8 distinct parent block numbers in increasing order; the last is always 16 - 1. `child_front_entries`: each front is symmetric positive definite. `parent_fronts`: each front is symmetric positive definite.
All inputs are finite; a program needn't handle non-finite values.
Results may differ from a plain program's by a relative error of at most 0.000078.
Values sent between devices are 32-bit elements; how exact they have to be, the bound alone decides.
A program may use at most 256 MiB of HBM per device.

v0:
```python
import jax
import jax.numpy as jnp
from jax import lax
from jax.sharding import PartitionSpec as P

B = 128
PIV = 1024
MOST = 4


def from_behind(block, axis, distance):
    devices = range(lax.axis_size(axis))
    route = [(i - distance, i) for i in devices if i - distance in devices]
    return lax.ppermute(block, axis, route)


def solve_rows(block_rows, diag_factor):
    return lax.linalg.triangular_solve(
        diag_factor, block_rows, left_side=False, lower=True, transpose_a=True
    )


def settle_blocks(blocks, block_ids, panel_no, diag_factor):
    shaped_ids = block_ids[:, None, None]
    kept = jnp.where(shaped_ids > panel_no, blocks, 0.0)
    return jnp.where(shaped_ids == panel_no, diag_factor[None], kept)


def partial_factor(front_rows, pivot_blocks, kept_blocks):
    front_row_count = lax.axis_size("rows")
    rows_index = lax.axis_index("rows")
    local_blocks = front_rows.shape[0]
    block_size = front_rows.shape[1]
    total_blocks = local_blocks * front_row_count
    pivot_width = pivot_blocks * block_size
    factor_cols = []
    whole_cols = []
    for panel_no in range(pivot_blocks):
        first_col = panel_no * block_size
        column_block = front_rows[:, :, first_col : first_col + block_size]
        if panel_no > 0:
            prior_self = jnp.concatenate(factor_cols, axis=2)
            prior_rows = jnp.concatenate(
                [whole_piece[first_col : first_col + block_size] for whole_piece in whole_cols],
                axis=1,
            )
            column_block = column_block - jnp.einsum(
                "awv,cv->awc", prior_self, prior_rows, precision=lax.Precision.HIGHEST
            )
        gathered = lax.all_gather(column_block[:, None], "rows", axis=1, tiled=True).reshape(
            total_blocks, block_size, block_size
        )
        diag_factor = jnp.linalg.cholesky(gathered[panel_no])
        factor_whole = solve_rows(gathered.reshape(-1, block_size), diag_factor).reshape(
            total_blocks, block_size, block_size
        )
        factor_whole = settle_blocks(
            factor_whole, jnp.arange(total_blocks, dtype=jnp.int32), panel_no, diag_factor
        )
        layered = factor_whole.reshape(local_blocks, front_row_count, block_size, block_size)
        self_front_factor = lax.dynamic_index_in_dim(layered, rows_index, 1, keepdims=False)
        factor_cols.append(self_front_factor)
        whole_cols.append(factor_whole.reshape(-1, block_size))
    self_cols = jnp.concatenate(factor_cols, axis=2)
    whole_factor = jnp.concatenate(whole_cols, axis=1)
    remaining = front_rows[kept_blocks:, :, pivot_width:] - jnp.einsum(
        "awv,cv->awc",
        self_cols[kept_blocks:],
        whole_factor[pivot_width:],
        precision=lax.Precision.HIGHEST,
    )
    return (self_cols, remaining)


def place_rows(update_rows, placement, local_blocks):
    front_row_count = lax.axis_size("rows")
    rows_index = lax.axis_index("rows")
    update_blocks = placement.shape[0]
    local_ids = jnp.arange(local_blocks, dtype=jnp.int32) * front_row_count + rows_index
    block_list = jnp.arange(update_blocks, dtype=jnp.int32)
    piece_rows = lax.all_gather(update_rows[:, None], "rows", axis=1, tiled=True)
    piece_count = piece_rows.shape[1]
    update_ids = (
        jnp.arange(piece_rows.shape[0], dtype=jnp.int32)[:, None] * front_row_count
        + jnp.arange(piece_count, dtype=jnp.int32)[None, :]
    )
    lookup = (update_ids[..., None] == block_list).astype(jnp.int32)
    target_block = jnp.sum(lookup * placement, axis=-1)
    row_onehot = (target_block[None] == local_ids[:, None, None]).astype(jnp.float32)
    return jnp.einsum("phm,hmic->pic", row_onehot, piece_rows, precision=lax.Precision.HIGHEST)


def place_columns(rows_placed, placement_float, front_order):
    local_blocks = rows_placed.shape[0]
    block_size = rows_placed.shape[1]
    update_blocks = placement_float.shape[0]
    col_onehot = (
        placement_float[:, None]
        == jnp.arange(front_order // block_size, dtype=jnp.int32).astype(jnp.float32)[None, :]
    ).astype(jnp.float32)
    shaped = rows_placed.reshape(local_blocks, block_size, update_blocks, block_size)
    placed = jnp.einsum("picb,cq->piqb", shaped, col_onehot, precision=lax.Precision.HIGHEST)
    return placed.reshape(local_blocks, block_size, front_order)


def on_device(child_front_entries, parent_fronts, parent_of, positions):
    front_row_count = lax.axis_size("rows")
    leaf_front_index = lax.axis_index("leaf")
    leaf_count = lax.axis_size("leaf")
    child_front_rows = child_front_entries[0, :, 0]
    local_blocks = child_front_rows.shape[0]
    front_order = child_front_rows.shape[2]
    pivot_blocks = PIV // B
    kept_blocks = pivot_blocks // front_row_count
    child_cols, update_rows = partial_factor(child_front_rows, pivot_blocks, kept_blocks)
    rows_placed = place_rows(update_rows, positions[0], local_blocks)
    own_places = positions[0].astype(jnp.float32)
    extended = place_columns(rows_placed, own_places, front_order)
    leaf_ids = jnp.arange(leaf_count, dtype=jnp.int32)
    previous = jnp.concatenate([jnp.full((1,), -1, jnp.int32), parent_of[:-1]])
    head_flags = (parent_of != previous).astype(jnp.float32)
    head_flag = jnp.sum(jnp.where(leaf_ids == leaf_front_index, head_flags, 0.0))
    own_parent = jnp.sum(jnp.where(leaf_ids == leaf_front_index, parent_of, 0))
    collected = extended
    for shift_no in range(1, MOST):
        next_rows, next_places = from_behind((rows_placed, own_places), "leaf", -shift_no)
        next_parent = jnp.sum(jnp.where(leaf_ids == leaf_front_index + shift_no, parent_of, 0))
        same_parent = (
            (next_parent == own_parent) & (leaf_front_index + shift_no < leaf_count)
        ).astype(jnp.float32)
        collected = collected + same_parent * place_columns(next_rows, next_places, front_order)
    assembled = parent_fronts[0, :, 0] + collected
    parent_cols, parent_rest = partial_factor(assembled, pivot_blocks, kept_blocks)
    parent_contribution_block = parent_rest * head_flag
    parent_cols = parent_cols * head_flag
    return (
        child_cols[None, :, None],
        parent_cols[None, :, None],
        parent_contribution_block[None, :, None],
    )


def solution(mesh):
    placed = (
        P("leaf", None, "rows", None, None),
        P("leaf", None, "rows", None, None),
        P(),
        P("leaf", None),
    )
    return jax.shard_map(
        on_device,
        mesh=mesh,
        in_specs=placed,
        out_specs=(
            P("leaf", None, "rows", None, None),
            P("leaf", None, "rows", None, None),
            P("leaf", None, "rows", None, None),
        ),
        check_vma=False,
    )
```

profile of v0, /device:TPU:0, one launch (start us, length us, event | category | flops | bytes accessed | tf_op | source)
XLA Modules:
  0.0 1130.7 jit_solution(9591443845841436315)
XLA Ops:
  10.4 19.2 %all-gather.35.cloned.1.call-done = f32[4,512,128]{2,1,0:T(8,128)} async-done(((f32[4,128,128]{2,1,0:T(8,128)}), f32[4,512,128]{2,1,0:T(8,128)}) %all-gather.35.cloned.1.call-update) | async-done | bytes 1048592 | tf_op jit(solution)/shard_map/all_gather | solution.py:50
  31.5 11.7 %cholesky.254 = f32[128,128]{1,0:T(8,128)S(1)} custom-call(f32[128,128]{1,0:T(8,128)S(1)} %fusion.111), custom_call_target="Cholesky" | custom-call | tf_op jit(solution)/shard_map/jit(cholesky)/cholesky | solution.py:53
  45.1 9.8 custom-call.20
  63.5 14.4 %all-gather.37.cloned.1.call-done = f32[4,512,128]{2,1,0:T(8,128)} async-done(((f32[4,128,128]{2,1,0:T(8,128)}), f32[4,512,128]{2,1,0:T(8,128)}) %all-gather.37.cloned.1.call-update) | async-done | bytes 1048592 | tf_op jit(solution)/shard_map/all_gather | solution.py:50
  79.9 11.7 %cholesky.265 = f32[128,128]{1,0:T(8,128)S(1)} custom-call(f32[128,128]{1,0:T(8,128)S(1)} %fusion.110), custom_call_target="Cholesky" | custom-call | tf_op jit(solution)/shard_map/jit(cholesky)/cholesky | solution.py:53
  94.0 11.3 custom-call.21
  115.5 16.1 %all-gather.39.cloned.1.call-done = f32[4,512,128]{2,1,0:T(8,128)} async-done(((f32[4,128,128]{2,1,0:T(8,128)}), f32[4,512,128]{2,1,0:T(8,128)}) %all-gather.39.cloned.1.call-update) | async-done | bytes 1048592 | tf_op jit(solution)/shard_map/all_gather | solution.py:50
  133.4 11.7 %cholesky.276 = f32[128,128]{1,0:T(8,128)S(1)} custom-call(f32[128,128]{1,0:T(8,128)S(1)} %fusion.109), custom_call_target="Cholesky" | custom-call | tf_op jit(solution)/shard_map/jit(cholesky)/cholesky | solution.py:53
  146.9 9.8 custom-call.22
  170.5 14.0 %all-gather.41.cloned.1.call-done = f32[4,512,128]{2,1,0:T(8,128)} async-done(((f32[4,128,128]{2,1,0:T(8,128)}), f32[4,512,128]{2,1,0:T(8,128)}) %all-gather.41.cloned.1.call-update) | async-done | bytes 1048592 | tf_op jit(solution)/shard_map/all_gather | solution.py:50
  186.3 11.7 %cholesky.287 = f32[128,128]{1,0:T(8,128)S(1)} custom-call(f32[128,128]{1,0:T(8,128)S(1)} %fusion.108), custom_call_target="Cholesky" | custom-call | tf_op jit(solution)/shard_map/jit(cholesky)/cholesky | solution.py:53
  199.9 9.8 custom-call.23
  238.6 11.7 %cholesky.298 = f32[128,128]{1,0:T(8,128)S(1)} custom-call(f32[128,128]{1,0:T(8,128)S(1)} %fusion.107), custom_call_target="Cholesky" | custom-call | tf_op jit(solution)/shard_map/jit(cholesky)/cholesky | solution.py:53
  252.1 9.8 custom-call.24
  274.3 16.2 %all-gather.45.cloned.1.call-done = f32[4,512,128]{2,1,0:T(8,128)} async-done(((f32[4,128,128]{2,1,0:T(8,128)}), f32[4,512,128]{2,1,0:T(8,128)}) %all-gather.45.cloned.1.call-update) | async-done | bytes 1048592 | tf_op jit(solution)/shard_map/all_gather | solution.py:50
  292.4 11.7 %cholesky.309 = f32[128,128]{1,0:T(8,128)S(1)} custom-call(f32[128,128]{1,0:T(8,128)S(1)} %fusion.106), custom_call_target="Cholesky" | custom-call | tf_op jit(solution)/shard_map/jit(cholesky)/cholesky | solution.py:53
  305.9 9.8 custom-call.25
  326.8 15.2 %all-gather.47.cloned.1.call-done = f32[4,512,128]{2,1,0:T(8,128)} async-done(((f32[4,128,128]{2,1,0:T(8,128)}), f32[4,512,128]{2,1,0:T(8,128)}) %all-gather.47.cloned.1.call-update) | async-done | bytes 1048592 | tf_op jit(solution)/shard_map/all_gather | solution.py:50
  343.9 11.7 %cholesky.320 = f32[128,128]{1,0:T(8,128)S(1)} custom-call(f32[128,128]{1,0:T(8,128)S(1)} %fusion.105), custom_call_target="Cholesky" | custom-call | tf_op jit(solution)/shard_map/jit(cholesky)/cholesky | solution.py:53
  357.4 9.8 custom-call.26
  381.6 16.5 %all-gather.49.cloned.1.call-done = f32[4,512,128]{2,1,0:T(8,128)} async-done(((f32[4,128,128]{2,1,0:T(8,128)}), f32[4,512,128]{2,1,0:T(8,128)}) %all-gather.49.cloned.1.call-update) | async-done | bytes 1048592 | tf_op jit(solution)/shard_map/all_gather | solution.py:50
  400.0 11.7 %cholesky.331 = f32[128,128]{1,0:T(8,128)S(1)} custom-call(f32[128,128]{1,0:T(8,128)S(1)} %fusion.104), custom_call_target="Cholesky" | custom-call | tf_op jit(solution)/shard_map/jit(cholesky)/cholesky | solution.py:53
  413.1 9.8 custom-call.27
  435.6 34.3 %all-gather.51.cloned.1.call-done = f32[2,512,1024]{2,1,0:T(8,128)} async-done(((f32[2,128,1024]{2,1,0:T(8,128)}), f32[2,512,1024]{2,1,0:T(8,128)}) %all-gather.51.cloned.1.call-update) | async-done | bytes 4194320 | tf_op jit(solution)/shard_map/all_gather | solution.py:81
  496.3 32.9 %collective-permute-done.3 = f32[4,128,1024]{2,0,1:T(4,128)} collective-permute-done((f32[4,128,1024]{2,0,1:T(4,128)S(1)}, f32[4,128,1024]{2,0,1:T(4,128)}, u32[]{:S(2)}, u32[]{:S(2)}) %collective-permute-start.3) | collective-permute-done | bytes 2097184 | tf_op jit(solution)/shard_map/ppermute | solution.py:14
  533.8 41.1 %collective-permute-done.1 = f32[4,128,1024]{2,0,1:T(4,128)} collective-permute-done((f32[4,128,1024]{2,0,1:T(4,128)S(1)}, f32[4,128,1024]{2,0,1:T(4,128)}, u32[]{:S(2)}, u32[]{:S(2)}) %collective-permute-start.1) | collective-permute-done | bytes 2097184 | tf_op jit(solution)/shard_map/ppermute | solution.py:14
  602.7 100.3 %all-gather.53.cloned.1.call-done = f32[4,512,128]{2,1,0:T(8,128)} async-done(((f32[4,128,128]{2,1,0:T(8,128)}), f32[4,512,128]{2,1,0:T(8,128)}) %all-gather.53.cloned.1.call-update) | async-done | bytes 1048592 | tf_op jit(solution)/shard_map/all_gather | solution.py:50
  704.9 11.7 %cholesky.342 = f32[128,128]{1,0:T(8,128)S(1)} custom-call(f32[128,128]{1,0:T(8,128)S(1)} %fusion.103), custom_call_target="Cholesky" | custom-call | tf_op jit(solution)/shard_map/jit(cholesky)/cholesky | solution.py:53
  718.4 9.8 custom-call.28
  738.1 15.7 %all-gather.55.cloned.1.call-done = f32[4,512,128]{2,1,0:T(8,128)} async-done(((f32[4,128,128]{2,1,0:T(8,128)}), f32[4,512,128]{2,1,0:T(8,128)}) %all-gather.55.cloned.1.call-update) | async-done | bytes 1048592 | tf_op jit(solution)/shard_map/all_gather | solution.py:50
  755.6 11.7 %cholesky.353 = f32[128,128]{1,0:T(8,128)S(1)} custom-call(f32[128,128]{1,0:T(8,128)S(1)} %fusion.102), custom_call_target="Cholesky" | custom-call | tf_op jit(solution)/shard_map/jit(cholesky)/cholesky | solution.py:53
  769.7 11.3 custom-call.29
  790.4 16.7 %all-gather.57.cloned.1.call-done = f32[4,512,128]{2,1,0:T(8,128)} async-done(((f32[4,128,128]{2,1,0:T(8,128)}), f32[4,512,128]{2,1,0:T(8,128)}) %all-gather.57.cloned.1.call-update) | async-done | bytes 1048592 | tf_op jit(solution)/shard_map/all_gather | solution.py:50
  808.9 11.7 %cholesky.364 = f32[128,128]{1,0:T(8,128)S(1)} custom-call(f32[128,128]{1,0:T(8,128)S(1)} %fusion.101), custom_call_target="Cholesky" | custom-call | tf_op jit(solution)/shard_map/jit(cholesky)/cholesky | solution.py:53
  822.4 9.8 custom-call.30
  843.9 15.5 %all-gather.59.cloned.1.call-done = f32[4,512,128]{2,1,0:T(8,128)} async-done(((f32[4,128,128]{2,1,0:T(8,128)}), f32[4,512,128]{2,1,0:T(8,128)}) %all-gather.59.cloned.1.call-update) | async-done | bytes 1048592 | tf_op jit(solution)/shard_map/all_gather | solution.py:50
  861.2 11.7 %cholesky.375 = f32[128,128]{1,0:T(8,128)S(1)} custom-call(f32[128,128]{1,0:T(8,128)S(1)} %fusion.100), custom_call_target="Cholesky" | custom-call | tf_op jit(solution)/shard_map/jit(cholesky)/cholesky | solution.py:53
  874.7 9.8 custom-call.31
  913.4 11.7 %cholesky.386 = f32[128,128]{1,0:T(8,128)S(1)} custom-call(f32[128,128]{1,0:T(8,128)S(1)} %fusion.99), custom_call_target="Cholesky" | custom-call | tf_op jit(solution)/shard_map/jit(cholesky)/cholesky | solution.py:53
  949.6 16.7 %all-gather.63.cloned.1.call-done = f32[4,512,128]{2,1,0:T(8,128)} async-done(((f32[4,128,128]{2,1,0:T(8,128)}), f32[4,512,128]{2,1,0:T(8,128)}) %all-gather.63.cloned.1.call-update) | async-done | bytes 1048592 | tf_op jit(solution)/shard_map/all_gather | solution.py:50
  968.1 11.7 %cholesky.397 = f32[128,128]{1,0:T(8,128)S(1)} custom-call(f32[128,128]{1,0:T(8,128)S(1)} %fusion.98), custom_call_target="Cholesky" | custom-call | tf_op jit(solution)/shard_map/jit(cholesky)/cholesky | solution.py:53
  982.2 10.6 custom-call.33
  1008.5 15.9 %all-gather.65.cloned.1.call-done = f32[4,512,128]{2,1,0:T(8,128)} async-done(((f32[4,128,128]{2,1,0:T(8,128)}), f32[4,512,128]{2,1,0:T(8,128)}) %all-gather.65.cloned.1.call-update) | async-done | bytes 1048592 | tf_op jit(solution)/shard_map/all_gather | solution.py:50
  1026.2 11.7 %cholesky.408 = f32[128,128]{1,0:T(8,128)S(1)} custom-call(f32[128,128]{1,0:T(8,128)S(1)} %fusion.97), custom_call_target="Cholesky" | custom-call | tf_op jit(solution)/shard_map/jit(cholesky)/cholesky | solution.py:53
  1040.4 10.6 custom-call.34
  1069.8 11.8 %all-gather.67.cloned.1.call-done = f32[4,512,128]{2,1,0:T(8,128)} async-done(((f32[4,128,128]{2,1,0:T(8,128)}), f32[4,512,128]{2,1,0:T(8,128)}) %all-gather.67.cloned.1.call-update) | async-done | bytes 1048592 | tf_op jit(solution)/shard_map/all_gather | solution.py:50
  1083.5 11.9 %cholesky.419 = f32[128,128]{1,0:T(8,128)S(1)} custom-call(f32[128,128]{1,0:T(8,128)S(1)} %fusion.96), custom_call_target="Cholesky" | custom-call | tf_op jit(solution)/shard_map/jit(cholesky)/cholesky | solution.py:53
  1096.9 9.8 custom-call.35
  (643 shorter events, 358.1 us)
Async XLA Ops:
  7.2 22.4 %all-gather.35.cloned.1.call-start = ((), (), s32[]{:S(2)}) async-start(), calls=%async_computation | async-start | bytes 1310720 | tf_op jit(solution)/shard_map/all_gather | solution.py:50
  8.9 69.1 %all-gather.37.cloned.1.call-start = ((), (), s32[]{:S(2)}) async-start(), calls=%async_computation.1 | async-start | bytes 1310720 | tf_op jit(solution)/shard_map/all_gather | solution.py:50
  10.2 48.4 %copy-start.98 = (pred[16]{0:T(512)(128)(4,1)}, pred[16]{0:T(512)(128)(4,1)S(1)}, u32[]{:S(2)}) copy-start(pred[16]{0:T(512)(128)(4,1)S(1)} %get-tuple-element.184) | copy-start | bytes 52
  10.2 48.4 %copy-start.100 = (pred[16]{0:T(512)(128)(4,1)}, pred[16]{0:T(512)(128)(4,1)S(1)}, u32[]{:S(2)}) copy-start(pred[16]{0:T(512)(128)(4,1)S(1)} %get-tuple-element.185) | copy-start | bytes 52
  61.1 70.5 %all-gather.39.cloned.1.call-start = ((), (), s32[]{:S(2)}) async-start(), calls=%async_computation.2 | async-start | bytes 1310720 | tf_op jit(solution)/shard_map/all_gather | solution.py:50
  114.7 69.8 %all-gather.41.cloned.1.call-start = ((), (), s32[]{:S(2)}) async-start(), calls=%async_computation.3 | async-start | bytes 1310720 | tf_op jit(solution)/shard_map/all_gather | solution.py:50
  115.2 46.9 %copy-start.102 = (pred[16]{0:T(512)(128)(4,1)}, pred[16]{0:T(512)(128)(4,1)S(1)}, u32[]{:S(2)}) copy-start(pred[16]{0:T(512)(128)(4,1)S(1)} %iota_compare_fusion.13) | copy-start | bytes 52
  115.2 46.9 %copy-start.104 = (pred[16]{0:T(512)(128)(4,1)}, pred[16]{0:T(512)(128)(4,1)S(1)}, u32[]{:S(2)}) copy-start(pred[16]{0:T(512)(128)(4,1)S(1)} %iota_compare_fusion.14) | copy-start | bytes 52
  115.3 99.8 %copy-start.92 = (pred[16]{0:T(512)(128)(4,1)}, pred[16]{0:T(512)(128)(4,1)S(1)}, u32[]{:S(2)}) copy-start(pred[16]{0:T(512)(128)(4,1)S(1)} %iota_compare_fusion.11) | copy-start | bytes 52
  115.3 99.8 %copy-start.94 = (pred[16]{0:T(512)(128)(4,1)}, pred[16]{0:T(512)(128)(4,1)S(1)}, u32[]{:S(2)}) copy-start(pred[16]{0:T(512)(128)(4,1)S(1)} %iota_compare_fusion.12) | copy-start | bytes 52
  115.4 48.0 %copy-start.80 = (pred[4,1]{1,0:T(4,128)(4,1)}, pred[4,1]{1,0:T(4,128)(4,1)S(1)}, u32[]{:S(2)}) copy-start(pred[4,1]{1,0:T(4,128)(4,1)S(1)} %get-tuple-element.191) | copy-start | bytes 16
  115.4 100.0 %copy-start.70 = (pred[4,1]{1,0:T(4,128)(4,1)}, pred[4,1]{1,0:T(4,128)(4,1)S(1)}, u32[]{:S(2)}) copy-start(pred[4,1]{1,0:T(4,128)(4,1)S(1)} %get-tuple-element.190) | copy-start | bytes 16
  115.5 44.5 %copy-start.40 = (pred[2048]{0:T(1024)(128)(4,1)}, pred[2048]{0:T(1024)(128)(4,1)S(1)}, u32[]{:S(2)}) copy-start(pred[2048]{0:T(1024)(128)(4,1)S(1)} %get-tuple-element.202) | copy-start | bytes 6148
  115.5 44.5 %copy-start.42 = (pred[2048]{0:T(1024)(128)(4,1)}, pred[2048]{0:T(1024)(128)(4,1)S(1)}, u32[]{:S(2)}) copy-start(pred[2048]{0:T(1024)(128)(4,1)S(1)} %get-tuple-element.203) | copy-start | bytes 6148
  167.7 69.1 %all-gather.43.cloned.1.call-start = ((), (), s32[]{:S(2)}) async-start(), calls=%async_computation.4 | async-start | bytes 1310720 | tf_op jit(solution)/shard_map/all_gather | solution.py:50
  168.5 46.8 %copy-start.82 = (pred[4,1]{1,0:T(4,128)(4,1)}, pred[4,1]{1,0:T(4,128)(4,1)S(1)}, u32[]{:S(2)}) copy-start(pred[4,1]{1,0:T(4,128)(4,1)S(1)} %get-tuple-element.197) | copy-start | bytes 16
  219.8 70.6 %all-gather.45.cloned.1.call-start = ((), (), s32[]{:S(2)}) async-start(), calls=%async_computation.5 | async-start | bytes 1310720 | tf_op jit(solution)/shard_map/all_gather | solution.py:50
  273.6 68.4 %all-gather.47.cloned.1.call-start = ((), (), s32[]{:S(2)}) async-start(), calls=%async_computation.6 | async-start | bytes 1310720 | tf_op jit(solution)/shard_map/all_gather | solution.py:50
  274.1 44.9 %copy-start.106 = (pred[16]{0:T(512)(128)(4,1)}, pred[16]{0:T(512)(128)(4,1)S(1)}, u32[]{:S(2)}) copy-start(pred[16]{0:T(512)(128)(4,1)S(1)} %iota_compare_fusion.7) | copy-start | bytes 52
  274.1 44.9 %copy-start.108 = (pred[16]{0:T(512)(128)(4,1)}, pred[16]{0:T(512)(128)(4,1)S(1)}, u32[]{:S(2)}) copy-start(pred[16]{0:T(512)(128)(4,1)S(1)} %iota_compare_fusion.8) | copy-start | bytes 52
  274.2 45.0 %copy-start.84 = (pred[4,1]{1,0:T(4,128)(4,1)}, pred[4,1]{1,0:T(4,128)(4,1)S(1)}, u32[]{:S(2)}) copy-start(pred[4,1]{1,0:T(4,128)(4,1)S(1)} %get-tuple-element.195) | copy-start | bytes 16
  274.2 98.3 %copy-start.72 = (pred[4,1]{1,0:T(4,128)(4,1)}, pred[4,1]{1,0:T(4,128)(4,1)S(1)}, u32[]{:S(2)}) copy-start(pred[4,1]{1,0:T(4,128)(4,1)S(1)} %get-tuple-element.194) | copy-start | bytes 16
  274.3 43.5 %copy-start.52 = (pred[2048]{0:T(1024)(128)(4,1)}, pred[2048]{0:T(1024)(128)(4,1)S(1)}, u32[]{:S(2)}) copy-start(pred[2048]{0:T(1024)(128)(4,1)S(1)} %get-tuple-element.208) | copy-start | bytes 6148
  274.3 43.5 %copy-start.54 = (pred[2048]{0:T(1024)(128)(4,1)}, pred[2048]{0:T(1024)(128)(4,1)S(1)}, u32[]{:S(2)}) copy-start(pred[2048]{0:T(1024)(128)(4,1)S(1)} %get-tuple-element.209) | copy-start | bytes 6148
  325.1 73.0 %all-gather.49.cloned.1.call-start = ((), (), s32[]{:S(2)}) async-start(), calls=%async_computation.7 | async-start | bytes 1310720 | tf_op jit(solution)/shard_map/all_gather | solution.py:50
  326.7 45.8 %copy-start.86 = (pred[4,1]{1,0:T(4,128)(4,1)}, pred[4,1]{1,0:T(4,128)(4,1)S(1)}, u32[]{:S(2)}) copy-start(pred[4,1]{1,0:T(4,128)(4,1)S(1)} %get-tuple-element.187) | copy-start | bytes 16
  326.7 99.4 %copy-start.74 = (pred[4,1]{1,0:T(4,128)(4,1)}, pred[4,1]{1,0:T(4,128)(4,1)S(1)}, u32[]{:S(2)}) copy-start(pred[4,1]{1,0:T(4,128)(4,1)S(1)} %get-tuple-element.186) | copy-start | bytes 16
  381.2 88.7 %all-gather.51.cloned.1.call-start = ((), (), s32[]{:S(2)}) async-start(), calls=%async_computation.8 | async-start | bytes 5242880 | tf_op jit(solution)/shard_map/all_gather | solution.py:81
  381.6 43.8 %copy-start.48 = (pred[2048]{0:T(1024)(128)(4,1)}, pred[2048]{0:T(1024)(128)(4,1)S(1)}, u32[]{:S(2)}) copy-start(pred[2048]{0:T(1024)(128)(4,1)S(1)} %get-tuple-element.212) | copy-start | bytes 6148
  381.6 43.8 %copy-start.50 = (pred[2048]{0:T(1024)(128)(4,1)}, pred[2048]{0:T(1024)(128)(4,1)S(1)}, u32[]{:S(2)}) copy-start(pred[2048]{0:T(1024)(128)(4,1)S(1)} %get-tuple-element.213) | copy-start | bytes 6148
  435.3 267.7 %all-gather.53.cloned.1.call-start = ((), (), s32[]{:S(2)}) async-start(), calls=%async_computation.9 | async-start | bytes 1310720 | tf_op jit(solution)/shard_map/all_gather | solution.py:50
  478.8 50.5 %collective-permute-start.3 = (f32[4,128,1024]{2,0,1:T(4,128)S(1)}, f32[4,128,1024]{2,0,1:T(4,128)}, u32[]{:S(2)}, u32[]{:S(2)}) collective-permute-start(f32[4,128,1024]{2,0,1:T(4,128)S(1)} %fusion.11), channel_id=1, source_target_pairs={{8,0},{12,4},{16,8},{20,12},{24,16},{28,20},{9,1},{13,5},{17,9},{2... | collective-permute-start | bytes 6291464 | tf_op jit(solution)/shard_map/ppermute | solution.py:14
  480.1 94.7 %collective-permute-start.1 = (f32[4,128,1024]{2,0,1:T(4,128)S(1)}, f32[4,128,1024]{2,0,1:T(4,128)}, u32[]{:S(2)}, u32[]{:S(2)}) collective-permute-start(f32[4,128,1024]{2,0,1:T(4,128)S(1)} %fusion.11), channel_id=1, source_target_pairs={{4,0},{8,4},{12,8},{16,12},{20,16},{24,20},{28,24},{5,1},{9,5},{13... | collective-permute-start | bytes 6291464 | tf_op jit(solution)/shard_map/ppermute | solution.py:14
  481.4 96.5 %collective-permute-start.5 = (f32[4,128,1024]{2,0,1:T(4,128)S(1)}, f32[4,128,1024]{2,0,1:T(4,128)}, u32[]{:S(2)}, u32[]{:S(2)}) collective-permute-start(f32[4,128,1024]{2,0,1:T(4,128)S(1)} %fusion.11), channel_id=1, source_target_pairs={{12,0},{16,4},{20,8},{24,12},{28,16},{13,1},{17,5},{21,9},{25,13},... | collective-permute-start | bytes 6291464 | tf_op jit(solution)/shard_map/ppermute | solution.py:14
  482.7 97.3 %collective-permute-start.2 = (f32[8]{0:T(128)S(1)}, f32[8]{0:T(128)S(1)}, u32[]{:S(2)}, u32[]{:S(2)}) collective-permute-start(f32[8]{0:T(128)S(1)} %bitcast_convert_fusion), channel_id=1, source_target_pairs={{8,0},{12,4},{16,8},{20,12},{24,16},{28,20},{9,1},{13,5},{17,9},{2... | collective-permute-start | bytes 104 | tf_op jit(solution)/shard_map/ppermute | solution.py:14
  484.0 99.8 %collective-permute-start = (f32[8]{0:T(128)S(1)}, f32[8]{0:T(128)S(1)}, u32[]{:S(2)}, u32[]{:S(2)}) collective-permute-start(f32[8]{0:T(128)S(1)} %bitcast_convert_fusion), channel_id=1, source_target_pairs={{4,0},{8,4},{12,8},{16,12},{20,16},{24,20},{28,24},{5,1},{9,5},{13... | collective-permute-start | bytes 104 | tf_op jit(solution)/shard_map/ppermute | solution.py:14
  529.3 56.6 %collective-permute-start.4 = (f32[8]{0:T(128)S(1)}, f32[8]{0:T(128)S(1)}, u32[]{:S(2)}, u32[]{:S(2)}) collective-permute-start(f32[8]{0:T(128)S(1)} %bitcast_convert_fusion), channel_id=1, source_target_pairs={{12,0},{16,4},{20,8},{24,12},{28,16},{13,1},{17,5},{21,9},{25,13},... | collective-permute-start | bytes 104 | tf_op jit(solution)/shard_map/ppermute | solution.py:14
  602.4 151.3 %all-gather.55.cloned.1.call-start = ((), (), s32[]{:S(2)}) async-start(), calls=%async_computation.10 | async-start | bytes 1310720 | tf_op jit(solution)/shard_map/all_gather | solution.py:50
  736.9 44.1 %copy-start.37 = (pred[2048]{0:T(1024)(128)(4,1)S(1)}, pred[2048]{0:T(1024)(128)(4,1)}, u32[]{:S(2)}) copy-start(pred[2048]{0:T(1024)(128)(4,1)} %copy-done.36) | copy-start | bytes 6148
  736.9 44.1 %copy-start.39 = (pred[2048]{0:T(1024)(128)(4,1)S(1)}, pred[2048]{0:T(1024)(128)(4,1)}, u32[]{:S(2)}) copy-start(pred[2048]{0:T(1024)(128)(4,1)} %copy-done.38) | copy-start | bytes 6148
  736.9 70.2 %all-gather.57.cloned.1.call-start = ((), (), s32[]{:S(2)}) async-start(), calls=%async_computation.11 | async-start | bytes 1310720 | tf_op jit(solution)/shard_map/all_gather | solution.py:50
  790.2 69.2 %all-gather.59.cloned.1.call-start = ((), (), s32[]{:S(2)}) async-start(), calls=%async_computation.12 | async-start | bytes 1310720 | tf_op jit(solution)/shard_map/all_gather | solution.py:50
  842.5 69.1 %all-gather.61.cloned.1.call-start = ((), (), s32[]{:S(2)}) async-start(), calls=%async_computation.13 | async-start | bytes 1310720 | tf_op jit(solution)/shard_map/all_gather | solution.py:50
  894.7 71.6 %all-gather.63.cloned.1.call-start = ((), (), s32[]{:S(2)}) async-start(), calls=%async_computation.14 | async-start | bytes 1310720 | tf_op jit(solution)/shard_map/all_gather | solution.py:50
  949.4 75.0 %all-gather.65.cloned.1.call-start = ((), (), s32[]{:S(2)}) async-start(), calls=%async_computation.15 | async-start | bytes 1310720 | tf_op jit(solution)/shard_map/all_gather | solution.py:50
  1007.5 43.6 %copy-start.57 = (pred[2048]{0:T(1024)(128)(4,1)S(1)}, pred[2048]{0:T(1024)(128)(4,1)}, u32[]{:S(2)}) copy-start(pred[2048]{0:T(1024)(128)(4,1)} %copy-done.56) | copy-start | bytes 6148
  1007.5 43.6 %copy-start.59 = (pred[2048]{0:T(1024)(128)(4,1)S(1)}, pred[2048]{0:T(1024)(128)(4,1)}, u32[]{:S(2)}) copy-start(pred[2048]{0:T(1024)(128)(4,1)} %copy-done.58) | copy-start | bytes 6148
  1007.5 74.1 %all-gather.67.cloned.1.call-start = ((), (), s32[]{:S(2)}) async-start(), calls=%async_computation.16 | async-start | bytes 1310720 | tf_op jit(solution)/shard_map/all_gather | solution.py:50
  (90 other events, 1252.1 us)
Sparse Core Ops, SparseCore 0:
  10.1 19.4 all-gather.34
  61.2 16.7 all-gather.36
  114.9 16.7 all-gather.38
  167.8 16.7 all-gather.40
  220.0 16.7 all-gather.42
  273.7 16.7 all-gather.44
  325.2 16.7 all-gather.46
  381.3 16.7 all-gather.48
  435.4 34.4 all-gather.50
  602.6 100.3 all-gather.52
  737.0 16.7 all-gather.54
  790.3 16.7 all-gather.56
  842.7 16.7 all-gather.58
  894.8 16.7 all-gather.60
  949.5 16.7 all-gather.62
  1007.6 16.7 all-gather.64
  1064.9 16.7 all-gather.66
where the time goes:
time: 1140 us; the launch traced here: 1130 us
  waiting for transfers between devices  432 us (38%)
  other arithmetic  426 us (37%)
  matrix products  124 us (11%)
  local copies, waits for them, and re-layouts  115 us (10%)
  between operations  20.6 us (2%)
  starting transfers between devices  12.2 us (1%)
    all_gather x16, waiting for transfers between devices, partial_factor(): lax.all_gather(column_block[:, None], 'rows', axis=1, tiled=True)  324 us
    another operation x48, other arithmetic, partial_factor(): diag_factor = jnp.linalg.cholesky(gathered[panel_no])  199 us
    another operation x32, other arithmetic, solve_rows(): lax.linalg.triangular_solve(diag_factor, block_rows, left_side=False, low...  175 us
    ppermute x6, waiting for transfers between devices, from_behind(): return lax.ppermute(block, axis, route)  74 us
    another operation x16, matrix products, solve_rows(): lax.linalg.triangular_solve(diag_factor, block_rows, left_side=False, low...  44.3 us
    dot_general x14, matrix products, partial_factor(): jnp.einsum('awv,cv->awc', prior_self, prior_rows, precision=lax.Precision...  39.9 us
    unnamed x278, local copies, waits for them, and re-layouts  35.5 us
    all_gather x1, waiting for transfers between devices, place_rows(): lax.all_gather(update_rows[:, None], 'rows', axis=1, tiled=True)  34.3 us
  transfers between devices with their start and end apart: 23, of which 19 were waited for; matrix products, arithmetic and copies ran while one was open for 4% of the time, Pallas kernels for 0%

commit v1 on v0

v1 whole, which is shorter than its diff:
```python
import functools

import jax
import jax.numpy as jnp
from jax import lax
from jax.experimental import pallas as pl
from jax.experimental.pallas import tpu as pltpu
from jax.sharding import PartitionSpec as P

B = 128
PIV = 1024
MOST = 4
SUB = 8
VMEM_LIMIT = 48 * 1024 * 1024


def from_behind(block, axis, distance):
    devices = range(lax.axis_size(axis))
    route = [(i - distance, i) for i in devices if i - distance in devices]
    return lax.ppermute(block, axis, route)


def dot_t(a, b):
    return lax.dot_general(
        a,
        b,
        (((1,), (1,)), ((), ())),
        precision=lax.Precision.HIGHEST,
        preferred_element_type=jnp.float32,
    )


def eliminate(block, upper_ref, inverse_ref):
    size = block.shape[0]
    groups = size // SUB
    lane = lax.broadcasted_iota(jnp.int32, (SUB, size), 1)
    sub = lax.broadcasted_iota(jnp.int32, (SUB, size), 0)
    left = [block[SUB * u : SUB * (u + 1), :] for u in range(groups)]
    right = [jnp.where(lane == sub + SUB * u, 1.0, 0.0) for u in range(groups)]
    sub_column = lax.broadcasted_iota(jnp.int32, (SUB, 1), 0)
    for j in range(size):
        t, s = divmod(j, SUB)
        row_left = left[t][s : s + 1, :]
        row_right = right[t][s : s + 1, :]
        pivot = row_left[:, j : j + 1]
        scale = lax.rsqrt(pivot)
        upper_ref[j : j + 1, :] = row_left * scale
        inverse_ref[j : j + 1, :] = row_right * scale
        over = 1.0 / pivot
        unit_left = row_left * over
        unit_right = row_right * over
        for u in range(t, groups):
            column = left[u][:, j : j + 1]
            if u == t:
                column = jnp.where(sub_column > s, column, 0.0)
            left[u] = left[u] - column * unit_left
            right[u] = right[u] - column * unit_right


def factor_kernel(pivot_ref, low_ref, out_ref, upper_ref, inverse_ref, *, chunk):
    width = pivot_ref.shape[0]
    total = out_ref.shape[0]
    panels = width // B
    chunks = total // chunk
    out_ref[:width, :] = pivot_ref[...]
    out_ref[width:, :] = low_ref[...]
    row = lax.broadcasted_iota(jnp.int32, (B, B), 0)
    col = lax.broadcasted_iota(jnp.int32, (B, B), 1)

    @pl.loop(0, panels)
    def _(k):
        first = pl.multiple_of(k * B, B)
        here = pl.ds(first, B)
        eliminate(out_ref[here, here], upper_ref, inverse_ref)
        inverse = inverse_ref[...]

        @pl.loop(lax.div(first, chunk), chunks)
        def _(c):
            rows = pl.ds(pl.multiple_of(c * chunk, chunk), chunk)
            out_ref[rows, here] = dot_t(out_ref[rows, here], inverse)

        out_ref[here, here] = jnp.where(row >= col, upper_ref[...].T, 0.0)

        @pl.loop(0, k)
        def _(i):
            out_ref[pl.ds(pl.multiple_of(i * B, B), B), here] = jnp.zeros((B, B), jnp.float32)

        @pl.loop(k + 1, panels)
        def _(j):
            there = pl.ds(pl.multiple_of(j * B, B), B)
            other = out_ref[there, here]

            @pl.loop(lax.div(j * B, chunk), chunks)
            def _(c):
                rows = pl.ds(pl.multiple_of(c * chunk, chunk), chunk)
                out_ref[rows, there] = out_ref[rows, there] - dot_t(out_ref[rows, here], other)


def factor_columns(pivot, low):
    width = pivot.shape[0]
    total = width + low.shape[0]
    chunk = 2 * B if total % (2 * B) == 0 else B
    return pl.pallas_call(
        functools.partial(factor_kernel, chunk=chunk),
        out_shape=jax.ShapeDtypeStruct((total, width), jnp.float32),
        in_specs=[pl.BlockSpec(memory_space=pltpu.VMEM)] * 2,
        out_specs=pl.BlockSpec(memory_space=pltpu.VMEM),
        scratch_shapes=[pltpu.VMEM((B, B), jnp.float32), pltpu.VMEM((B, B), jnp.float32)],
        compiler_params=pltpu.CompilerParams(vmem_limit_bytes=VMEM_LIMIT),
        cost_estimate=pl.CostEstimate(
            flops=100_000_000_000, bytes_accessed=2 * 4 * total * width, transcendentals=0
        ),
        name="factor_columns",
    )(pivot, low)


def update_kernel(index_ref, valid_ref, low_ref, entries_ref, out_ref):
    count = out_ref.shape[0]
    width = out_ref.shape[2]
    step = 2 * B
    for p in range(count):
        rows = pl.ds(pl.multiple_of(index_ref[p] * B, B), B)
        valid = valid_ref[p]

        @pl.when(valid == 0)
        def _():
            out_ref[p] = jnp.zeros(out_ref.shape[1:], jnp.float32)

        @pl.when(valid != 0)
        def _():
            @pl.loop(0, width // step)
            def _(c):
                cols = pl.ds(pl.multiple_of(c * step, step), step)
                out_ref[p, :, cols] = entries_ref[rows, cols] - dot_t(low_ref[rows, :], low_ref[cols, :])


def placed_update(index, valid, low, entries):
    count = index.shape[0]
    smem = pl.BlockSpec(memory_space=pltpu.SMEM)
    vmem = pl.BlockSpec(memory_space=pltpu.VMEM)
    return pl.pallas_call(
        update_kernel,
        out_shape=jax.ShapeDtypeStruct((count, B, entries.shape[1]), jnp.float32),
        in_specs=[smem, smem, vmem, vmem],
        out_specs=vmem,
        compiler_params=pltpu.CompilerParams(vmem_limit_bytes=VMEM_LIMIT),
        cost_estimate=pl.CostEstimate(
            flops=6 * 2 * count * B * entries.shape[1] * low.shape[1],
            bytes_accessed=4 * 2 * low.size,
            transcendentals=0,
        ),
        name="placed_update",
    )(index, valid, low, entries)


def assemble_kernel(places_ref, flags_ref, base_ref, *refs):
    pieces, out_ref = refs[:-1], refs[-1]
    out_ref[...] = base_ref[...]
    for n, piece in enumerate(pieces):

        @pl.when(flags_ref[n] != 0)
        def _():
            for b in range(piece.shape[2] // B):
                cols = pl.ds(pl.multiple_of(places_ref[n, b] * B, B), B)
                out_ref[:, :, cols] = out_ref[:, :, cols] + piece[:, :, b * B : (b + 1) * B]


def assemble(places, flags, base, pieces):
    smem = pl.BlockSpec(memory_space=pltpu.SMEM)
    vmem = pl.BlockSpec(memory_space=pltpu.VMEM)
    return pl.pallas_call(
        assemble_kernel,
        out_shape=jax.ShapeDtypeStruct(base.shape, jnp.float32),
        in_specs=[smem, smem, vmem] + [vmem] * len(pieces),
        out_specs=vmem,
        compiler_params=pltpu.CompilerParams(vmem_limit_bytes=VMEM_LIMIT),
        cost_estimate=pl.CostEstimate(flops=base.size, bytes_accessed=16 * base.size, transcendentals=0),
        name="assemble",
    )(places, flags, base, *pieces)


def gather_rows(blocks):
    whole = lax.all_gather(blocks[:, None], "rows", axis=1, tiled=True)
    return whole.reshape(-1, blocks.shape[-1])


def own_rows(factor, kept):
    ranks = lax.axis_size("rows")
    width = factor.shape[1]
    top = factor[:width].reshape(kept, ranks, B, width)
    top = lax.dynamic_index_in_dim(top, lax.axis_index("rows"), 1, keepdims=False)
    return jnp.concatenate([top, factor[width:].reshape(kept, B, width)], axis=0)


def on_device(child_front_entries, parent_fronts, parent_of, positions):
    ranks = lax.axis_size("rows")
    rank = lax.axis_index("rows")
    leaf = lax.axis_index("leaf")
    leaves = lax.axis_size("leaf")
    child = child_front_entries[0, :, 0]
    parent = parent_fronts[0, :, 0]
    blocks = child.shape[0]
    kept = PIV // B // ranks

    pivot = gather_rows(child[:kept, :, :PIV])
    entries = gather_rows(child[kept:, :, PIV:])
    low = child[kept:, :, :PIV].reshape(-1, PIV)
    child_factor = factor_columns(pivot, low)
    low_whole = gather_rows(child_factor[PIV:].reshape(kept, B, PIV))

    own = positions[0]
    ids = jnp.arange(blocks, dtype=jnp.int32) * ranks + rank
    match = (ids[:, None] == own[None, :]).astype(jnp.int32)
    valid = jnp.sum(match, axis=1)
    index = jnp.sum(match * jnp.arange(own.shape[0], dtype=jnp.int32)[None, :], axis=1)

    leaf_ids = jnp.arange(leaves, dtype=jnp.int32)
    parent_at = lambda n: jnp.sum(jnp.where(leaf_ids == n, parent_of, 0))
    own_parent = parent_at(leaf)
    is_head = (leaf == 0) | (parent_at(leaf - 1) != own_parent)
    flags = [jnp.int32(1)]
    places = [own]
    for shift in range(1, MOST):
        same = (parent_at(leaf + shift) == own_parent) & (leaf + shift < leaves)
        flags.append(same.astype(jnp.int32))
        places.append(from_behind(own.astype(jnp.float32), "leaf", -shift).astype(jnp.int32))
    flags = jnp.stack(flags)
    places = jnp.stack(places)

    def shifted(update):
        return [update] + [from_behind(update, "leaf", -shift) for shift in range(1, MOST)]

    top_pieces = shifted(placed_update(index[:kept], valid[:kept], low_whole, entries))
    rest_pieces = shifted(placed_update(index[kept:], valid[kept:], low_whole, entries))
    top = assemble(places, flags, parent[:kept], top_pieces)
    parent_pivot = gather_rows(top[:, :, :PIV])
    rest = assemble(places, flags, parent[kept:], rest_pieces)
    parent_factor = factor_columns(parent_pivot, rest[:, :, :PIV].reshape(-1, PIV))
    parent_own = parent_factor[PIV:]
    parent_whole = gather_rows(parent_own.reshape(kept, B, PIV))
    contribution = rest[:, :, PIV:] - dot_t(parent_own, parent_whole).reshape(kept, B, -1)
    return (
        own_rows(child_factor, kept)[None, :, None],
        jnp.where(is_head, own_rows(parent_factor, kept), 0.0)[None, :, None],
        jnp.where(is_head, contribution, 0.0)[None, :, None],
    )


def solution(mesh):
    placed = (
        P("leaf", None, "rows", None, None),
        P("leaf", None, "rows", None, None),
        P(),
        P("leaf", None),
    )
    return jax.shard_map(
        on_device,
        mesh=mesh,
        in_specs=placed,
        out_specs=(
            P("leaf", None, "rows", None, None),
            P("leaf", None, "rows", None, None),
            P("leaf", None, "rows", None, None),
        ),
        check_vma=False,
    )
```

time: 1140 us -> 595 us (0.52)
  other arithmetic: 426 us -> 4.02 us
  Pallas kernels: 0 us -> 265 us
  waiting for transfers between devices: 432 us -> 258 us
  matrix products: 124 us -> 4.7 us
  local copies, waits for them, and re-layouts: 115 us -> 30.5 us
    another operation x80 -> x5, other arithmetic: 373 us -> 0.1 us  [the longest x1 0.08 us: on_device(): flags = jnp.stack(flags)]
    pallas_call x0 -> x6, Pallas kernels: none -> 265 us  [the longest x2 240 us: factor_columns(): pl.pallas_call(functools.partial(factor_kernel, chunk=chunk), out_shape=j...]
    all_gather x17 -> x5, waiting for transfers between devices: 358 us -> 150 us  [gather_rows(): whole = lax.all_gather(blocks[:, None], 'rows', axis=1, tiled=True)]
    dot_general x21 -> x1, matrix products: 79.5 us -> 4.7 us  [dot_t(): lax.dot_general(a, b, (((1,), (1,)), ((), ())), precision=lax.Precision.H...]
    another operation x16 -> x0, matrix products: 44.3 us -> none  [solve_rows(): lax.linalg.triangular_solve(diag_factor, block_rows, left_side=False, low...]
    reshape x34 -> x0, local copies, waits for them, and re-layouts: 36.6 us -> none  [the longest x30 26.6 us: partial_factor(): solve_rows(gathered.reshape(-1, block_size), diag_factor)]
    ppermute x6 -> x9, waiting for transfers between devices: 74 us -> 108 us  [from_behind(): return lax.ppermute(block, axis, route)]
    unnamed x278 -> x20, local copies, waits for them, and re-layouts: 35.5 us -> 9.2 us
  transfers between devices with their start and end apart: 23 -> 14, of which waited for: 19 -> 6; matrix products, arithmetic and copies ran while one was open for 4% -> 2% of each run, Pallas kernels for 0% -> 24%
where the time goes in v1:
time: 595 us; the launch traced here: 593 us
  Pallas kernels  265 us (45%)
  waiting for transfers between devices  258 us (43%)
  local copies, waits for them, and re-layouts  30.5 us (5%)
  between operations  18.8 us (3%)
  starting transfers between devices  12 us (2%)
    pallas_call x2, Pallas kernels, factor_columns(): pl.pallas_call(functools.partial(factor_kernel, chunk=chunk), out_shape=j...  240 us
    all_gather x5, waiting for transfers between devices, gather_rows(): whole = lax.all_gather(blocks[:, None], 'rows', axis=1, tiled=True)  150 us
    ppermute x9, waiting for transfers between devices, from_behind(): return lax.ppermute(block, axis, route)  108 us
    pallas_call x2, Pallas kernels, placed_update(): pl.pallas_call(update_kernel, out_shape=jax.ShapeDtypeStruct((count, B, e...  18.6 us
  transfers between devices with their start and end apart: 14, of which 6 were waited for; matrix products, arithmetic and copies ran while one was open for 2% of the time, Pallas kernels for 24%

profile of v1, /device:TPU:0, one launch (start us, length us, event | category | flops | bytes accessed | tf_op | source)
XLA Modules:
  0.0 593.4 jit_solution(16911366266823872818)
XLA Ops:
  7.2 3.5 fusion.9
  10.8 0.0 all-gather.15.cloned.1.call-start
  10.8 0.7 all-gather.15.cloned.1.call-update
  11.6 36.5 %all-gather.13.cloned.1.call-done = f32[2,512,1024]{2,1,0:T(8,128)} async-done(((f32[2,128,1024]{2,1,0:T(8,128)}), f32[2,512,1024]{2,1,0:T(8,128)}) %all-gather.13.cloned.1.call-update) | async-done | bytes 4194320 | tf_op jit(solution)/shard_map/all_gather | solution.py:183
  48.1 2.2 copy-done.3
  50.3 119.9 %factor_columns.2 = f32[1280,1024]{1,0:T(8,128)} custom-call(f32[1024,1024]{1,0:T(8,128)S(1)} %bitcast.55, f32[256,1024]{1,0:T(8,128)S(1)} %bitcast.51), custom_call_target="tpu_custom_call" | custom-call | flops 99999997952 | bytes 10485760 | tf_op jit(solution)/shard_map/factor_columns/pallas_call | solution.py:103
  170.2 2.3 slice.77
  172.5 0.0 all-gather.17.cloned.1.call-start
  172.6 1.3 collective-permute-start.2
  173.9 1.3 collective-permute-start.1
  175.2 0.2 fusion.3
  175.4 0.1 fusion.10
  175.5 31.7 %all-gather.9.cloned.1.call-done = f32[2,4,128,1024]{3,2,1,0:T(8,128)} async-done(((f32[2,1,128,1024]{3,2,1,0:T(8,128)}), f32[2,4,128,1024]{3,2,1,0:T(8,128)}) %all-gather.9.cloned.1.call-update) | async-done | bytes 4194320 | tf_op jit(solution)/shard_map/all_gather | solution.py:183
  207.2 2.2 copy-done
  209.3 11.7 %placed_update.2.refs_0_ = f32[2,128,1024]{2,1,0:T(8,128)S(1)} custom-call(s32[2]{0:T(128)S(1)} %get-tuple-element.28.index_ref, s32[2]{0:T(128)S(1)} %get-tuple-element.25.valid_ref, f32[1024,1024]{1,0:T(8,128)S(1)} %bitcast.52, f32[1024,1024]{1,0:T(8,128)} %bitcast.67), custom_call_target="tpu_custom_call" | custom-call | flops 3221225472 | bytes 8388608 | tf_op jit(solution)/shard_map/placed_update/pallas_call | solution.py:141
  221.0 1.3 collective-permute-start.5
  222.3 1.3 collective-permute-start.4
  223.6 1.3 collective-permute-start.3
  224.9 2.5 slice_bitcast_fusion
  227.4 0.8 fusion.4
  231.8 0.1 add_convert_fusion.flags_ref
  231.9 1.3 collective-permute-start
  233.2 29.4 %collective-permute-done = f32[8]{0:T(128)S(1)} collective-permute-done((f32[8]{0:T(128)S(1)}, f32[8]{0:T(128)S(1)}, u32[]{:S(2)}, u32[]{:S(2)}) %collective-permute-start) | collective-permute-done | bytes 64 | tf_op jit(solution)/shard_map/ppermute | solution.py:20
  262.6 10.0 %collective-permute-done.4.refs_2_ = f32[2,128,1024]{2,1,0:T(8,128)S(1)} collective-permute-done((f32[2,128,1024]{2,1,0:T(8,128)S(1)}, f32[2,128,1024]{2,1,0:T(8,128)S(1)}, u32[]{:S(2)}, u32[]{:S(2)}) %collective-permute-start.4) | collective-permute-done | bytes 1048608 | tf_op jit(solution)/shard_map/ppermute | solution.py:20
  272.7 3.6 assemble.2
  276.3 2.3 slice.80
  278.6 2.2 copy-done.1
  280.8 6.9 %placed_update.3.refs_0_ = f32[2,128,1024]{2,1,0:T(8,128)S(1)} custom-call(s32[2]{0:T(128)S(1)} %get-tuple-element.29.index_ref, s32[2]{0:T(128)S(1)} %get-tuple-element.24.valid_ref, f32[1024,1024]{1,0:T(8,128)S(1)} %bitcast.53, f32[1024,1024]{1,0:T(8,128)} %bitcast.68), custom_call_target="tpu_custom_call" | custom-call | flops 3221225472 | bytes 8388608 | tf_op jit(solution)/shard_map/placed_update/pallas_call | solution.py:141
  287.7 1.3 collective-permute-start.8
  289.0 1.3 collective-permute-start.7
  290.3 1.5 collective-permute-start.6
  291.8 68.3 %collective-permute-done.8.refs_3_ = f32[2,128,1024]{2,1,0:T(8,128)S(1)} collective-permute-done((f32[2,128,1024]{2,1,0:T(8,128)S(1)}, f32[2,128,1024]{2,1,0:T(8,128)S(1)}, u32[]{:S(2)}, u32[]{:S(2)}) %collective-permute-start.8) | collective-permute-done | bytes 1048608 | tf_op jit(solution)/shard_map/ppermute | solution.py:20
  360.1 3.4 assemble.3
  363.5 1.3 slice.82
  364.8 2.2 copy-done.2
  367.0 119.9 %factor_columns.3 = f32[1280,1024]{1,0:T(8,128)} custom-call(f32[1024,1024]{1,0:T(8,128)S(1)} %bitcast.54, f32[256,1024]{1,0:T(8,128)S(1)} %bitcast.50), custom_call_target="tpu_custom_call" | custom-call | flops 99999997952 | bytes 10485760 | tf_op jit(solution)/shard_map/factor_columns/pallas_call | solution.py:103
  486.8 2.3 slice.84
  490.4 2.2 slice-done.1
  492.5 0.1 dynamic-slice_bitcast_fusion.1
  492.6 0.2 copy-done.5
  492.8 1.5 maximum_bitcast_fusion
  494.3 2.2 slice-done
  496.5 0.1 dynamic-slice_bitcast_fusion
  496.6 0.2 copy-done.4
  496.8 1.5 maximum_select_fusion
  498.3 81.4 %all-gather.11.cloned.1.call-done = f32[2,4,128,1024]{3,2,0,1:T(8,128)} async-done(((f32[2,1,128,1024]{3,2,0,1:T(8,128)}), f32[2,4,128,1024]{3,2,0,1:T(8,128)}) %all-gather.11.cloned.1.call-update) | async-done | bytes 4194320 | tf_op jit(solution)/shard_map/all_gather | solution.py:183
  579.6 2.5 copy.23
  582.2 4.7 fusion.1
  (37 shorter events, 0.3 us)
Async XLA Ops:
  7.2 40.9 %all-gather.13.cloned.1.call-start = ((), (), s32[]{:S(2)}) async-start(), calls=%async_computation.2 | async-start | bytes 5242880 | tf_op jit(solution)/shard_map/all_gather | solution.py:183
  10.8 164.7 %all-gather.15.cloned.1.call-start = ((), (), s32[]{:S(2)}) async-start(), calls=%async_computation.3 | async-start | bytes 5242880 | tf_op jit(solution)/shard_map/all_gather | solution.py:183
  11.5 195.6 %all-gather.9.cloned.1.call-start = ((), (), s32[]{:S(2)}) async-start(), calls=%async_computation | async-start | bytes 5242880 | tf_op jit(solution)/shard_map/all_gather | solution.py:183
  48.1 2.2 copy-start.3
  50.3 122.3 %copy-start.8 = (s32[1,8]{1,0:T(1,128)S(1)}, s32[1,8]{1,0:T(1,128)}, u32[]{:S(2)}) copy-start(s32[1,8]{1,0:T(1,128)} %param.7) | copy-start | bytes 100
  172.5 192.3 %all-gather.17.cloned.1.call-start = ((), (), s32[]{:S(2)}) async-start(), calls=%async_computation.4 | async-start | bytes 5242880 | tf_op jit(solution)/shard_map/all_gather | solution.py:183
  172.6 59.3 %collective-permute-start.2 = (f32[8]{0:T(128)S(1)}, f32[8]{0:T(128)S(1)}, u32[]{:S(2)}, u32[]{:S(2)}) collective-permute-start(f32[8]{0:T(128)S(1)} %bitcast_convert_fusion), channel_id=1, source_target_pairs={{12,0},{16,4},{20,8},{24,12},{28,16},{13,1},{17,5},{21,9},{25,13},... | collective-permute-start | bytes 104 | tf_op jit(solution)/shard_map/ppermute | solution.py:20
  173.9 59.3 %collective-permute-start.1 = (f32[8]{0:T(128)S(1)}, f32[8]{0:T(128)S(1)}, u32[]{:S(2)}, u32[]{:S(2)}) collective-permute-start(f32[8]{0:T(128)S(1)} %bitcast_convert_fusion), channel_id=1, source_target_pairs={{8,0},{12,4},{16,8},{20,12},{24,16},{28,20},{9,1},{13,5},{17,9},{2... | collective-permute-start | bytes 104 | tf_op jit(solution)/shard_map/ppermute | solution.py:20
  207.2 2.2 copy-start
  209.3 15.6 %copy-start.7 = (f32[1,4,1,128,2048]{4,3,2,1,0:T(8,128)S(1)}, f32[1,4,1,128,2048]{4,3,2,1,0:T(8,128)}, u32[]{:S(2)}) copy-start(f32[1,4,1,128,2048]{4,3,2,1,0:T(8,128)} %param.5) | copy-start | bytes 12582916
  221.0 41.6 %collective-permute-start.5 = (f32[2,128,1024]{2,1,0:T(8,128)S(1)}, f32[2,128,1024]{2,1,0:T(8,128)S(1)}, u32[]{:S(2)}, u32[]{:S(2)}) collective-permute-start(f32[2,128,1024]{2,1,0:T(8,128)S(1)} %placed_update.2.refs_0_), channel_id=1, source_target_pairs={{12,0},{16,4},{20,8},{24,12},{28,16},{13,1},{17,5},{21,9},{25,13},... | collective-permute-start | bytes 3145736 | tf_op jit(solution)/shard_map/ppermute | solution.py:20
  222.3 50.4 %collective-permute-start.4 = (f32[2,128,1024]{2,1,0:T(8,128)S(1)}, f32[2,128,1024]{2,1,0:T(8,128)S(1)}, u32[]{:S(2)}, u32[]{:S(2)}) collective-permute-start(f32[2,128,1024]{2,1,0:T(8,128)S(1)} %placed_update.2.refs_0_), channel_id=1, source_target_pairs={{8,0},{12,4},{16,8},{20,12},{24,16},{28,20},{9,1},{13,5},{17,9},{2... | collective-permute-start | bytes 3145736 | tf_op jit(solution)/shard_map/ppermute | solution.py:20
  223.6 49.1 %collective-permute-start.3 = (f32[2,128,1024]{2,1,0:T(8,128)S(1)}, f32[2,128,1024]{2,1,0:T(8,128)}, u32[]{:S(2)}, u32[]{:S(2)}) collective-permute-start(f32[2,128,1024]{2,1,0:T(8,128)S(1)} %placed_update.2.refs_0_), channel_id=1, source_target_pairs={{4,0},{8,4},{12,8},{16,12},{20,16},{24,20},{28,24},{5,1},{9,5},{13... | collective-permute-start | bytes 3145736 | tf_op jit(solution)/shard_map/ppermute | solution.py:20
  224.9 2.5 copy-start.9
  231.9 30.7 %collective-permute-start = (f32[8]{0:T(128)S(1)}, f32[8]{0:T(128)S(1)}, u32[]{:S(2)}, u32[]{:S(2)}) collective-permute-start(f32[8]{0:T(128)S(1)} %bitcast_convert_fusion), channel_id=1, source_target_pairs={{4,0},{8,4},{12,8},{16,12},{20,16},{24,20},{28,24},{5,1},{9,5},{13... | collective-permute-start | bytes 104 | tf_op jit(solution)/shard_map/ppermute | solution.py:20
  278.6 301.1 %all-gather.11.cloned.1.call-start = ((), (), s32[]{:S(2)}) async-start(), calls=%async_computation.1 | async-start | bytes 5242880 | tf_op jit(solution)/shard_map/all_gather | solution.py:183
  278.6 2.2 copy-start.1
  287.7 72.4 %collective-permute-start.8 = (f32[2,128,1024]{2,1,0:T(8,128)S(1)}, f32[2,128,1024]{2,1,0:T(8,128)S(1)}, u32[]{:S(2)}, u32[]{:S(2)}) collective-permute-start(f32[2,128,1024]{2,1,0:T(8,128)S(1)} %placed_update.3.refs_0_), channel_id=1, source_target_pairs={{12,0},{16,4},{20,8},{24,12},{28,16},{13,1},{17,5},{21,9},{25,13},... | collective-permute-start | bytes 3145736 | tf_op jit(solution)/shard_map/ppermute | solution.py:20
  289.0 71.1 %collective-permute-start.7 = (f32[2,128,1024]{2,1,0:T(8,128)S(1)}, f32[2,128,1024]{2,1,0:T(8,128)S(1)}, u32[]{:S(2)}, u32[]{:S(2)}) collective-permute-start(f32[2,128,1024]{2,1,0:T(8,128)S(1)} %placed_update.3.refs_0_), channel_id=1, source_target_pairs={{8,0},{12,4},{16,8},{20,12},{24,16},{28,20},{9,1},{13,5},{17,9},{2... | collective-permute-start | bytes 3145736 | tf_op jit(solution)/shard_map/ppermute | solution.py:20
  290.3 69.8 %collective-permute-start.6 = (f32[2,128,1024]{2,1,0:T(8,128)S(1)}, f32[2,128,1024]{2,1,0:T(8,128)S(1)}, u32[]{:S(2)}, u32[]{:S(2)}) collective-permute-start(f32[2,128,1024]{2,1,0:T(8,128)S(1)} %placed_update.3.refs_0_), channel_id=1, source_target_pairs={{4,0},{8,4},{12,8},{16,12},{20,16},{24,20},{28,24},{5,1},{9,5},{13... | collective-permute-start | bytes 3145736 | tf_op jit(solution)/shard_map/ppermute | solution.py:20
  364.8 2.2 copy-start.2
  490.4 2.2 slice-start.1
  490.4 2.5 copy-start.5
  494.3 2.2 slice-start
  494.3 2.5 copy-start.4
  498.3 83.9 %copy-start.6 = (f32[2,128,2048]{2,1,0:T(8,128)S(1)}, f32[2,128,2048]{2,1,0:T(8,128)}, u32[]{:S(2)}) copy-start(f32[2,128,2048]{2,1,0:T(8,128)} %assemble.3) | copy-start | bytes 6291460
Sparse Core Ops, SparseCore 0:
  10.9 37.1 all-gather.12
  50.2 34.5 all-gather.14
  172.6 34.4 all-gather.8
  278.7 72.0 all-gather.16
  489.3 90.3 all-gather.10

commit v2 on v1

--- a/solution.py
+++ b/solution.py
@@ -11,6 +11,7 @@
 PIV = 1024
 MOST = 4
 SUB = 8
+STEP = 4
 VMEM_LIMIT = 48 * 1024 * 1024
 
 
@@ -37,33 +38,48 @@
     sub = lax.broadcasted_iota(jnp.int32, (SUB, size), 0)
     left = [block[SUB * u : SUB * (u + 1), :] for u in range(groups)]
     right = [jnp.where(lane == sub + SUB * u, 1.0, 0.0) for u in range(groups)]
-    sub_column = lax.broadcasted_iota(jnp.int32, (SUB, 1), 0)
-    for j in range(size):
+    full = lambda x: jnp.broadcast_to(x, (SUB, size))
+    for j in range(0, size, STEP):
         t, s = divmod(j, SUB)
-        row_left = left[t][s : s + 1, :]
-        row_right = right[t][s : s + 1, :]
-        pivot = row_left[:, j : j + 1]
-        scale = lax.rsqrt(pivot)
-        upper_ref[j : j + 1, :] = row_left * scale
-        inverse_ref[j : j + 1, :] = row_right * scale
-        over = 1.0 / pivot
-        unit_left = row_left * over
-        unit_right = row_right * over
-        for u in range(t, groups):
-            column = left[u][:, j : j + 1]
-            if u == t:
-                column = jnp.where(sub_column > s, column, 0.0)
-            left[u] = left[u] - column * unit_left
-            right[u] = right[u] - column * unit_right
-
-
-def factor_kernel(pivot_ref, low_ref, out_ref, upper_ref, inverse_ref, *, chunk):
+        columns = [full(left[t][:, j + i : j + i + 1]) for i in range(STEP)]
+        unit_left, unit_right, across = [], [], []
+        for i in range(STEP):
+            row_left = left[t][s + i : s + i + 1, :]
+            row_right = right[t][s + i : s + i + 1, :]
+            pivot = columns[i][s + i : s + i + 1, :]
+            scale = lax.rsqrt(pivot)
+            upper_ref[j + i : j + i + 1, :] = row_left * scale
+            inverse_ref[j + i : j + i + 1, :] = row_right * scale
+            over = 1.0 / pivot
+            unit_left.append(full(row_left * over))
+            unit_right.append(full(row_right * over))
+            across.append(
+                [full(columns[i][s + n : s + n + 1, :] * over) if n > i else None for n in range(STEP)]
+            )
+            below = jnp.where(sub > s + i, columns[i], 0.0)
+            left[t] = left[t] - below * unit_left[i]
+            right[t] = right[t] - below * unit_right[i]
+            for n in range(i + 1, STEP):
+                columns[n] = columns[n] - below * across[i][n]
+        for u in range(t + 1, groups):
+            columns = [full(left[u][:, j + i : j + i + 1]) for i in range(STEP)]
+            for i in range(STEP):
+                left[u] = left[u] - columns[i] * unit_left[i]
+                right[u] = right[u] - columns[i] * unit_right[i]
+                for n in range(i + 1, STEP):
+                    columns[n] = columns[n] - columns[i] * across[i][n]
+
+
+def factor_kernel(*refs, chunk):
+    pivot_ref, low_refs = refs[0], refs[1:-4]
+    out_ref, inverses_ref, upper_ref, inverse_ref = refs[-4:]
     width = pivot_ref.shape[0]
     total = out_ref.shape[0]
     panels = width // B
     chunks = total // chunk
     out_ref[:width, :] = pivot_ref[...]
-    out_ref[width:, :] = low_ref[...]
+    for low_ref in low_refs:
+        out_ref[width:, :] = low_ref[...]
     row = lax.broadcasted_iota(jnp.int32, (B, B), 0)
     col = lax.broadcasted_iota(jnp.int32, (B, B), 1)
 
@@ -73,6 +89,7 @@
         here = pl.ds(first, B)
         eliminate(out_ref[here, here], upper_ref, inverse_ref)
         inverse = inverse_ref[...]
+        inverses_ref[here, :] = inverse
 
         @pl.loop(lax.div(first, chunk), chunks)
         def _(c):
@@ -96,22 +113,50 @@
                 out_ref[rows, there] = out_ref[rows, there] - dot_t(out_ref[rows, here], other)
 
 
-def factor_columns(pivot, low):
+def factor_columns(pivot, *low):
     width = pivot.shape[0]
-    total = width + low.shape[0]
+    total = width + sum(rows.shape[0] for rows in low)
     chunk = 2 * B if total % (2 * B) == 0 else B
+    vmem = pl.BlockSpec(memory_space=pltpu.VMEM)
     return pl.pallas_call(
         functools.partial(factor_kernel, chunk=chunk),
-        out_shape=jax.ShapeDtypeStruct((total, width), jnp.float32),
-        in_specs=[pl.BlockSpec(memory_space=pltpu.VMEM)] * 2,
-        out_specs=pl.BlockSpec(memory_space=pltpu.VMEM),
+        out_shape=(
+            jax.ShapeDtypeStruct((total, width), jnp.float32),
+            jax.ShapeDtypeStruct((width, B), jnp.float32),
+        ),
+        in_specs=[vmem] * (1 + len(low)),
+        out_specs=(vmem, vmem),
         scratch_shapes=[pltpu.VMEM((B, B), jnp.float32), pltpu.VMEM((B, B), jnp.float32)],
         compiler_params=pltpu.CompilerParams(vmem_limit_bytes=VMEM_LIMIT),
         cost_estimate=pl.CostEstimate(
             flops=100_000_000_000, bytes_accessed=2 * 4 * total * width, transcendentals=0
         ),
         name="factor_columns",
-    )(pivot, low)
+    )(pivot, *low)
+
+
+def solve_kernel(factor_ref, inverses_ref, low_ref, out_ref):
+    for first in range(0, factor_ref.shape[1], B):
+        here = slice(first, first + B)
+        rest = low_ref[:, here]
+        if first > 0:
+            rest = rest - dot_t(out_ref[:, :first], factor_ref[here, :first])
+        out_ref[:, here] = dot_t(rest, inverses_ref[here, :])
+
+
+def solve_low(factor, inverses, low):
+    vmem = pl.BlockSpec(memory_space=pltpu.VMEM)
+    return pl.pallas_call(
+        solve_kernel,
+        out_shape=jax.ShapeDtypeStruct(low.shape, jnp.float32),
+        in_specs=[vmem] * 3,
+        out_specs=vmem,
+        compiler_params=pltpu.CompilerParams(vmem_limit_bytes=VMEM_LIMIT),
+        cost_estimate=pl.CostEstimate(
+            flops=6 * low.size * low.shape[1], bytes_accessed=4 * factor.size, transcendentals=0
+        ),
+        name="solve_low",
+    )(factor, inverses, low)
 
 
 def update_kernel(index_ref, valid_ref, low_ref, entries_ref, out_ref):
@@ -154,7 +199,7 @@
 
 
 def assemble_kernel(places_ref, flags_ref, base_ref, *refs):
-    pieces, out_ref = refs[:-1], refs[-1]
+    pieces, out_ref = refs[:MOST], refs[-1]
     out_ref[...] = base_ref[...]
     for n, piece in enumerate(pieces):
 
@@ -165,18 +210,18 @@
                 out_ref[:, :, cols] = out_ref[:, :, cols] + piece[:, :, b * B : (b + 1) * B]
 
 
-def assemble(places, flags, base, pieces):
+def assemble(places, flags, base, pieces, *after):
     smem = pl.BlockSpec(memory_space=pltpu.SMEM)
     vmem = pl.BlockSpec(memory_space=pltpu.VMEM)
     return pl.pallas_call(
         assemble_kernel,
         out_shape=jax.ShapeDtypeStruct(base.shape, jnp.float32),
-        in_specs=[smem, smem, vmem] + [vmem] * len(pieces),
+        in_specs=[smem, smem, vmem] + [vmem] * len(pieces) + [pl.BlockSpec(memory_space=pl.ANY)] * len(after),
         out_specs=vmem,
         compiler_params=pltpu.CompilerParams(vmem_limit_bytes=VMEM_LIMIT),
         cost_estimate=pl.CostEstimate(flops=base.size, bytes_accessed=16 * base.size, transcendentals=0),
         name="assemble",
-    )(places, flags, base, *pieces)
+    )(places, flags, base, *pieces, *after)
 
 
 def gather_rows(blocks):
@@ -184,12 +229,11 @@
     return whole.reshape(-1, blocks.shape[-1])
 
 
-def own_rows(factor, kept):
-    ranks = lax.axis_size("rows")
-    width = factor.shape[1]
-    top = factor[:width].reshape(kept, ranks, B, width)
+def own_rows(top, low, kept):
+    width = top.shape[1]
+    top = top.reshape(kept, -1, B, width)
     top = lax.dynamic_index_in_dim(top, lax.axis_index("rows"), 1, keepdims=False)
-    return jnp.concatenate([top, factor[width:].reshape(kept, B, width)], axis=0)
+    return jnp.concatenate([top, low.reshape(kept, B, width)], axis=0)
 
 
 def on_device(child_front_entries, parent_fronts, parent_of, positions):
@@ -205,7 +249,7 @@
     pivot = gather_rows(child[:kept, :, :PIV])
     entries = gather_rows(child[kept:, :, PIV:])
     low = child[kept:, :, :PIV].reshape(-1, PIV)
-    child_factor = factor_columns(pivot, low)
+    child_factor, _ = factor_columns(pivot, low)
     low_whole = gather_rows(child_factor[PIV:].reshape(kept, B, PIV))
 
     own = positions[0]
@@ -234,14 +278,14 @@
     rest_pieces = shifted(placed_update(index[kept:], valid[kept:], low_whole, entries))
     top = assemble(places, flags, parent[:kept], top_pieces)
     parent_pivot = gather_rows(top[:, :, :PIV])
-    rest = assemble(places, flags, parent[kept:], rest_pieces)
-    parent_factor = factor_columns(parent_pivot, rest[:, :, :PIV].reshape(-1, PIV))
-    parent_own = parent_factor[PIV:]
+    parent_top, inverses = factor_columns(parent_pivot)
+    rest = assemble(places, flags, parent[kept:], rest_pieces, inverses)
+    parent_own = solve_low(parent_top, inverses, rest[:, :, :PIV].reshape(-1, PIV))
     parent_whole = gather_rows(parent_own.reshape(kept, B, PIV))
     contribution = rest[:, :, PIV:] - dot_t(parent_own, parent_whole).reshape(kept, B, -1)
     return (
-        own_rows(child_factor, kept)[None, :, None],
-        jnp.where(is_head, own_rows(parent_factor, kept), 0.0)[None, :, None],
+        own_rows(child_factor[:PIV], child_factor[PIV:], kept)[None, :, None],
+        jnp.where(is_head, own_rows(parent_top, parent_own, kept), 0.0)[None, :, None],
         jnp.where(is_head, contribution, 0.0)[None, :, None],
     )
 

time: 595 us -> 433 us (0.73)
  Pallas kernels: 265 us -> 160 us
  waiting for transfers between devices: 258 us -> 203 us
    pallas_call x2 -> x3, Pallas kernels: 240 us -> 139 us  [the longest x2 128 us: factor_columns(): pl.pallas_call(functools.partial(factor_kernel, chunk=chunk), out_shape=(...]
    ppermute x9, waiting for transfers between devices: 108 us -> 38.8 us  [from_behind(): return lax.ppermute(block, axis, route)]
    all_gather x5, waiting for transfers between devices: 150 us -> 163 us  [gather_rows(): whole = lax.all_gather(blocks[:, None], 'rows', axis=1, tiled=True)]
  transfers between devices with their start and end apart: 14 -> 14, of which waited for: 6 -> 5; matrix products, arithmetic and copies ran while one was open for 2% -> 3% of each run, Pallas kernels for 24% -> 33%
where the time goes in v2:
time: 433 us
  waiting for transfers between devices  203 us (47%)
  Pallas kernels  160 us (37%)
  local copies, waits for them, and re-layouts  27.1 us (6%)
  between operations  19.3 us (4%)
  starting transfers between devices  12 us (3%)
  matrix products  5.92 us (1%)
  other arithmetic  5.3 us (1%)
    all_gather x5, waiting for transfers between devices, gather_rows(): whole = lax.all_gather(blocks[:, None], 'rows', axis=1, tiled=True)  163 us
    pallas_call x2, Pallas kernels, factor_columns(): pl.pallas_call(functools.partial(factor_kernel, chunk=chunk), out_shape=(...  128 us
    ppermute x9, waiting for transfers between devices, from_behind(): return lax.ppermute(block, axis, route)  38.8 us
    pallas_call x2, Pallas kernels, placed_update(): pl.pallas_call(update_kernel, out_shape=jax.ShapeDtypeStruct((count, B, e...  13.9 us
    ppermute x9, starting transfers between devices, from_behind(): return lax.ppermute(block, axis, route)  11.8 us
    pallas_call x1, Pallas kernels, solve_low(): pl.pallas_call(solve_kernel, out_shape=jax.ShapeDtypeStruct(low.shape, jn...  10.2 us
  transfers between devices with their start and end apart: 14, of which 5 were waited for; matrix products, arithmetic and copies ran while one was open for 3% of the time, Pallas kernels for 33%

profile of v2, /device:TPU:0, one launch (start us, length us, event | category | flops | bytes accessed | tf_op | source)
XLA Modules:
  0.0 432.7 jit_solution(3033228349822865422)
XLA Ops:
  7.2 0.0 all-gather.13.cloned.1.call-start
  7.2 3.5 fusion.9
  10.7 0.0 all-gather.13.cloned.1.call-update
  10.8 0.0 all-gather.15.cloned.1.call-start
  10.8 0.7 all-gather.15.cloned.1.call-update
  11.5 0.0 all-gather.9.cloned.1.call-start
  11.6 36.5 %all-gather.13.cloned.1.call-done = f32[2,512,1024]{2,1,0:T(8,128)} async-done(((f32[2,128,1024]{2,1,0:T(8,128)}), f32[2,512,1024]{2,1,0:T(8,128)}) %all-gather.13.cloned.1.call-update) | async-done | bytes 4194320 | tf_op jit(solution)/shard_map/all_gather | solution.py:228
  48.1 2.2 copy-done.3
  50.3 69.5 %factor_columns.2 = (f32[1280,1024]{1,0:T(8,128)}, f32[1024,128]{1,0:T(8,128)}) custom-call(f32[1024,1024]{1,0:T(8,128)S(1)} %bitcast.55, f32[256,1024]{1,0:T(8,128)S(1)} %bitcast.52), custom_call_target="tpu_custom_call" | custom-call | flops 99999997952 | bytes 10485760 | tf_op jit(solution)/shard_map/factor_columns/pallas_call | solution.py:121
  119.8 2.3 slice.52
  122.1 0.0 all-gather.17.cloned.1.call-start
  122.2 1.3 collective-permute-start.2
  123.5 1.3 collective-permute-start.1
  124.8 0.2 fusion.3
  125.0 0.1 fusion.10
  125.1 31.7 %all-gather.9.cloned.1.call-done = f32[2,4,128,1024]{3,2,1,0:T(8,128)} async-done(((f32[2,1,128,1024]{3,2,1,0:T(8,128)}), f32[2,4,128,1024]{3,2,1,0:T(8,128)}) %all-gather.9.cloned.1.call-update) | async-done | bytes 4194320 | tf_op jit(solution)/shard_map/all_gather | solution.py:228
  156.8 2.2 copy-done.1
  158.9 7.0 %placed_update.2.refs_0_ = f32[2,128,1024]{2,1,0:T(8,128)S(1)} custom-call(s32[2]{0:T(128)S(1)} %get-tuple-element.34.index_ref, s32[2]{0:T(128)S(1)} %get-tuple-element.31.valid_ref, f32[1024,1024]{1,0:T(8,128)S(1)} %bitcast.53, f32[1024,1024]{1,0:T(8,128)} %bitcast.63), custom_call_target="tpu_custom_call" | custom-call | flops 3221225472 | bytes 8388608 | tf_op jit(solution)/shard_map/placed_update/pallas_call | solution.py:186
  166.0 1.3 collective-permute-start.5
  167.3 1.3 collective-permute-start.4
  168.6 1.3 collective-permute-start.3
  169.9 2.5 slice_bitcast_fusion
  172.4 0.8 fusion.4
  177.2 0.1 add_convert_fusion.flags_ref
  177.3 1.3 collective-permute-start
  178.6 38.8 %collective-permute-done = f32[8]{0:T(128)S(1)} collective-permute-done((f32[8]{0:T(128)S(1)}, f32[8]{0:T(128)S(1)}, u32[]{:S(2)}, u32[]{:S(2)}) %collective-permute-start) | collective-permute-done | bytes 64 | tf_op jit(solution)/shard_map/ppermute | solution.py:21
  217.4 3.8 assemble.2
  221.3 2.3 slice.69
  223.6 0.0 all-gather.11.cloned.1.call-start
  223.7 2.2 copy-done.2
  225.9 6.9 %placed_update.3.refs_0_ = f32[2,128,1024]{2,1,0:T(8,128)S(1)} custom-call(s32[2]{0:T(128)S(1)} %get-tuple-element.35.index_ref, s32[2]{0:T(128)S(1)} %get-tuple-element.30.valid_ref, f32[1024,1024]{1,0:T(8,128)S(1)} %bitcast.54, f32[1024,1024]{1,0:T(8,128)} %bitcast.64), custom_call_target="tpu_custom_call" | custom-call | flops 3221225472 | bytes 8388608 | tf_op jit(solution)/shard_map/placed_update/pallas_call | solution.py:186
  232.8 1.3 collective-permute-start.8
  234.1 1.3 collective-permute-start.7
  235.4 1.5 collective-permute-start.6
  236.8 63.3 %all-gather.17.cloned.1.call-done = f32[2,512,1024]{2,1,0:T(8,128)} async-done(((f32[2,128,1024]{2,1,0:T(8,128)}), f32[2,512,1024]{2,1,0:T(8,128)}) %all-gather.17.cloned.1.call-update) | async-done | bytes 4194320 | tf_op jit(solution)/shard_map/all_gather | solution.py:228
  300.2 59.0 %factor_columns.3 = (f32[1024,1024]{1,0:T(8,128)S(1)}, f32[1024,128]{1,0:T(8,128)S(1)}) custom-call(f32[1024,1024]{1,0:T(8,128)} %bitcast.65), custom_call_target="tpu_custom_call" | custom-call | flops 99999997952 | bytes 8388608 | tf_op jit(solution)/shard_map/factor_columns/pallas_call | solution.py:121
  359.2 2.0 copy-done
  361.2 3.8 assemble.3
  365.0 1.3 slice.71
  366.4 10.2 %solve_low.1 = f32[256,1024]{1,0:T(8,128)} custom-call(f32[1024,1024]{1,0:T(8,128)} %copy-done, f32[1024,128]{1,0:T(8,128)S(1)} %get-tuple-element.8.refs_4_.inverses_ref, f32[256,1024]{1,0:T(8,128)S(1)} %bitcast.51), custom_call_target="tpu_custom_call" | custom-call | flops 1610612736 | bytes 4194304 | tf_op jit(solution)/shard_map/solve_low/pallas_call | solution.py:149
  377.9 2.6 slice.51
  380.5 0.1 dynamic-slice_bitcast_fusion.1
  380.6 1.5 maximum_bitcast_fusion
  382.0 1.3 dynamic-slice_bitcast_fusion
  383.3 2.8 maximum_select_fusion
  386.1 31.7 %all-gather.11.cloned.1.call-done = f32[2,4,128,1024]{3,2,0,1:T(8,128)} async-done(((f32[2,1,128,1024]{3,2,0,1:T(8,128)}), f32[2,4,128,1024]{3,2,0,1:T(8,128)}) %all-gather.11.cloned.1.call-update) | async-done | bytes 4194320 | tf_op jit(solution)/shard_map/all_gather | solution.py:228
  417.8 2.5 copy.23
  420.3 5.9 %fusion.1 = f32[1,2,1,128,1024]{4,3,2,1,0:T(8,128)} fusion(f32[2,128,2048]{2,1,0:T(8,128)S(1)} %copy-done.5, pred[]{:T(512)S(6)} %or.3, f32[2,128,1024]{2,1,0:T(8,128)} %bitcast.28, f32[1024,1024,1]{1,0,2:T(8,128)S(1)} %bitcast.56), kind=kOutput, calls=%fused_computation.6 | convolution fusion | flops 3221749760 | bytes 7340033 | tf_op jit(solution)/shard_map/dot_general | solution.py:25
  (32 shorter events, 0.1 us)
Async XLA Ops:
  7.2 40.9 %all-gather.13.cloned.1.call-start = ((), (), s32[]{:S(2)}) async-start(), calls=%async_computation.2 | async-start | bytes 5242880 | tf_op jit(solution)/shard_map/all_gather | solution.py:228
  10.8 114.3 %all-gather.15.cloned.1.call-start = ((), (), s32[]{:S(2)}) async-start(), calls=%async_computation.3 | async-start | bytes 5242880 | tf_op jit(solution)/shard_map/all_gather | solution.py:228
  11.5 145.2 %all-gather.9.cloned.1.call-start = ((), (), s32[]{:S(2)}) async-start(), calls=%async_computation | async-start | bytes 5242880 | tf_op jit(solution)/shard_map/all_gather | solution.py:228
  48.1 2.2 copy-start.3
  50.3 71.9 %copy-start.7 = (s32[1,8]{1,0:T(1,128)S(1)}, s32[1,8]{1,0:T(1,128)}, u32[]{:S(2)}) copy-start(s32[1,8]{1,0:T(1,128)} %param.7) | copy-start | bytes 100
  122.1 178.0 %all-gather.17.cloned.1.call-start = ((), (), s32[]{:S(2)}) async-start(), calls=%async_computation.4 | async-start | bytes 5242880 | tf_op jit(solution)/shard_map/all_gather | solution.py:228
  122.2 55.1 %collective-permute-start.2 = (f32[8]{0:T(128)S(1)}, f32[8]{0:T(128)S(1)}, u32[]{:S(2)}, u32[]{:S(2)}) collective-permute-start(f32[8]{0:T(128)S(1)} %bitcast_convert_fusion), channel_id=1, source_target_pairs={{12,0},{16,4},{20,8},{24,12},{28,16},{13,1},{17,5},{21,9},{25,13},... | collective-permute-start | bytes 104 | tf_op jit(solution)/shard_map/ppermute | solution.py:21
  123.5 55.1 %collective-permute-start.1 = (f32[8]{0:T(128)S(1)}, f32[8]{0:T(128)S(1)}, u32[]{:S(2)}, u32[]{:S(2)}) collective-permute-start(f32[8]{0:T(128)S(1)} %bitcast_convert_fusion), channel_id=1, source_target_pairs={{8,0},{12,4},{16,8},{20,12},{24,16},{28,20},{9,1},{13,5},{17,9},{2... | collective-permute-start | bytes 104 | tf_op jit(solution)/shard_map/ppermute | solution.py:21
  156.7 2.2 copy-start.1
  158.9 11.0 %copy-start.6 = (f32[1,4,1,128,2048]{4,3,2,1,0:T(8,128)S(1)}, f32[1,4,1,128,2048]{4,3,2,1,0:T(8,128)}, u32[]{:S(2)}) copy-start(f32[1,4,1,128,2048]{4,3,2,1,0:T(8,128)} %param.5) | copy-start | bytes 12582916
  166.0 51.4 %collective-permute-start.5 = (f32[2,128,1024]{2,1,0:T(8,128)S(1)}, f32[2,128,1024]{2,1,0:T(8,128)S(1)}, u32[]{:S(2)}, u32[]{:S(2)}) collective-permute-start(f32[2,128,1024]{2,1,0:T(8,128)S(1)} %placed_update.2.refs_0_), channel_id=1, source_target_pairs={{12,0},{16,4},{20,8},{24,12},{28,16},{13,1},{17,5},{21,9},{25,13},... | collective-permute-start | bytes 3145736 | tf_op jit(solution)/shard_map/ppermute | solution.py:21
  167.3 50.1 %collective-permute-start.4 = (f32[2,128,1024]{2,1,0:T(8,128)S(1)}, f32[2,128,1024]{2,1,0:T(8,128)S(1)}, u32[]{:S(2)}, u32[]{:S(2)}) collective-permute-start(f32[2,128,1024]{2,1,0:T(8,128)S(1)} %placed_update.2.refs_0_), channel_id=1, source_target_pairs={{8,0},{12,4},{16,8},{20,12},{24,16},{28,20},{9,1},{13,5},{17,9},{2... | collective-permute-start | bytes 3145736 | tf_op jit(solution)/shard_map/ppermute | solution.py:21
  168.6 48.8 %collective-permute-start.3 = (f32[2,128,1024]{2,1,0:T(8,128)S(1)}, f32[2,128,1024]{2,1,0:T(8,128)}, u32[]{:S(2)}, u32[]{:S(2)}) collective-permute-start(f32[2,128,1024]{2,1,0:T(8,128)S(1)} %placed_update.2.refs_0_), channel_id=1, source_target_pairs={{4,0},{8,4},{12,8},{16,12},{20,16},{24,20},{28,24},{5,1},{9,5},{13... | collective-permute-start | bytes 3145736 | tf_op jit(solution)/shard_map/ppermute | solution.py:21
  169.9 2.5 copy-start.8
  177.3 40.1 %collective-permute-start = (f32[8]{0:T(128)S(1)}, f32[8]{0:T(128)S(1)}, u32[]{:S(2)}, u32[]{:S(2)}) collective-permute-start(f32[8]{0:T(128)S(1)} %bitcast_convert_fusion), channel_id=1, source_target_pairs={{4,0},{8,4},{12,8},{16,12},{20,16},{24,20},{28,24},{5,1},{9,5},{13... | collective-permute-start | bytes 104 | tf_op jit(solution)/shard_map/ppermute | solution.py:21
  223.6 194.2 %all-gather.11.cloned.1.call-start = ((), (), s32[]{:S(2)}) async-start(), calls=%async_computation.1 | async-start | bytes 5242880 | tf_op jit(solution)/shard_map/all_gather | solution.py:228
  223.7 2.2 copy-start.2
  232.8 128.4 %collective-permute-start.8 = (f32[2,128,1024]{2,1,0:T(8,128)S(1)}, f32[2,128,1024]{2,1,0:T(8,128)S(1)}, u32[]{:S(2)}, u32[]{:S(2)}) collective-permute-start(f32[2,128,1024]{2,1,0:T(8,128)S(1)} %placed_update.3.refs_0_), channel_id=1, source_target_pairs={{12,0},{16,4},{20,8},{24,12},{28,16},{13,1},{17,5},{21,9},{25,13},... | collective-permute-start | bytes 3145736 | tf_op jit(solution)/shard_map/ppermute | solution.py:21
  234.1 127.1 %collective-permute-start.7 = (f32[2,128,1024]{2,1,0:T(8,128)S(1)}, f32[2,128,1024]{2,1,0:T(8,128)S(1)}, u32[]{:S(2)}, u32[]{:S(2)}) collective-permute-start(f32[2,128,1024]{2,1,0:T(8,128)S(1)} %placed_update.3.refs_0_), channel_id=1, source_target_pairs={{8,0},{12,4},{16,8},{20,12},{24,16},{28,20},{9,1},{13,5},{17,9},{2... | collective-permute-start | bytes 3145736 | tf_op jit(solution)/shard_map/ppermute | solution.py:21
  235.4 125.8 %collective-permute-start.6 = (f32[2,128,1024]{2,1,0:T(8,128)S(1)}, f32[2,128,1024]{2,1,0:T(8,128)}, u32[]{:S(2)}, u32[]{:S(2)}) collective-permute-start(f32[2,128,1024]{2,1,0:T(8,128)S(1)} %placed_update.3.refs_0_), channel_id=1, source_target_pairs={{4,0},{8,4},{12,8},{16,12},{20,16},{24,20},{28,24},{5,1},{9,5},{13... | collective-permute-start | bytes 3145736 | tf_op jit(solution)/shard_map/ppermute | solution.py:21
  359.2 2.0 copy-start
  377.9 2.7 copy-start.4
  386.1 34.2 %copy-start.5 = (f32[2,128,2048]{2,1,0:T(8,128)S(1)}, f32[2,128,2048]{2,1,0:T(8,128)}, u32[]{:S(2)}) copy-start(f32[2,128,2048]{2,1,0:T(8,128)} %assemble.3) | copy-start | bytes 6291460
Sparse Core Ops, SparseCore 0:
  10.9 37.1 all-gather.12
  50.2 34.5 all-gather.14
  122.2 34.4 all-gather.8
  223.7 76.3 all-gather.16
  376.8 40.9 all-gather.10

commit v3 on v2

--- a/solution.py
+++ b/solution.py
@@ -11,7 +11,7 @@
 PIV = 1024
 MOST = 4
 SUB = 8
-STEP = 4
+STEP = 8
 VMEM_LIMIT = 48 * 1024 * 1024
 
 

time: 433 us -> 421 us (0.972)
  Pallas kernels: 160 us -> 144 us
    pallas_call x2, Pallas kernels: 128 us -> 111 us  [factor_columns(): pl.pallas_call(functools.partial(factor_kernel, chunk=chunk), out_shape=(...]
  transfers between devices with their start and end apart: 14 -> 14, of which waited for: 5 -> 6; matrix products, arithmetic and copies ran while one was open for 3% -> 3% of each run, Pallas kernels for 33% -> 30%
where the time goes in v3:
time: 421 us; the launch traced here: 420 us
  waiting for transfers between devices  207 us (49%)
  Pallas kernels  144 us (34%)
  local copies, waits for them, and re-layouts  27.1 us (6%)
  between operations  19.3 us (5%)
  starting transfers between devices  12 us (3%)
  matrix products  5.92 us (1%)
  other arithmetic  5.3 us (1%)
    all_gather x5, waiting for transfers between devices, gather_rows(): whole = lax.all_gather(blocks[:, None], 'rows', axis=1, tiled=True)  167 us
    pallas_call x2, Pallas kernels, factor_columns(): pl.pallas_call(functools.partial(factor_kernel, chunk=chunk), out_shape=(...  111 us
    ppermute x9, waiting for transfers between devices, from_behind(): return lax.ppermute(block, axis, route)  38.7 us
    pallas_call x2, Pallas kernels, placed_update(): pl.pallas_call(update_kernel, out_shape=jax.ShapeDtypeStruct((count, B, e...  13.9 us
    ppermute x9, starting transfers between devices, from_behind(): return lax.ppermute(block, axis, route)  11.8 us
    pallas_call x1, Pallas kernels, solve_low(): pl.pallas_call(solve_kernel, out_shape=jax.ShapeDtypeStruct(low.shape, jn...  10.2 us
    pallas_call x2, Pallas kernels, assemble(): pl.pallas_call(assemble_kernel, out_shape=jax.ShapeDtypeStruct(base.shape...  8.71 us
    unnamed x18, local copies, waits for them, and re-layouts  8.59 us
  transfers between devices with their start and end apart: 14, of which 6 were waited for; matrix products, arithmetic and copies ran while one was open for 3% of the time, Pallas kernels for 30%

profile of v3, /device:TPU:0, one launch (start us, length us, event | category | flops | bytes accessed | tf_op | source)
XLA Modules:
  0.0 420.2 jit_solution(6859576997465010811)
XLA Ops:
  7.2 0.0 all-gather.13.cloned.1.call-start
  7.2 3.5 fusion.9
  10.8 0.0 all-gather.15.cloned.1.call-start
  10.8 0.7 all-gather.15.cloned.1.call-update
  11.5 0.0 all-gather.9.cloned.1.call-start
  11.6 36.5 %all-gather.13.cloned.1.call-done = f32[2,512,1024]{2,1,0:T(8,128)} async-done(((f32[2,128,1024]{2,1,0:T(8,128)}), f32[2,512,1024]{2,1,0:T(8,128)}) %all-gather.13.cloned.1.call-update) | async-done | bytes 4194320 | tf_op jit(solution)/shard_map/all_gather | solution.py:228
  48.1 2.2 copy-done.3
  50.3 60.6 %factor_columns.2 = (f32[1280,1024]{1,0:T(8,128)}, f32[1024,128]{1,0:T(8,128)}) custom-call(f32[1024,1024]{1,0:T(8,128)S(1)} %bitcast.55, f32[256,1024]{1,0:T(8,128)S(1)} %bitcast.52), custom_call_target="tpu_custom_call" | custom-call | flops 99999997952 | bytes 10485760 | tf_op jit(solution)/shard_map/factor_columns/pallas_call | solution.py:121
  110.9 2.3 slice.52
  113.3 0.0 all-gather.17.cloned.1.call-start
  113.3 1.3 collective-permute-start.2
  114.6 1.3 collective-permute-start.1
  116.0 0.2 fusion.3
  116.1 0.1 fusion.10
  116.2 31.7 %all-gather.9.cloned.1.call-done = f32[2,4,128,1024]{3,2,1,0:T(8,128)} async-done(((f32[2,1,128,1024]{3,2,1,0:T(8,128)}), f32[2,4,128,1024]{3,2,1,0:T(8,128)}) %all-gather.9.cloned.1.call-update) | async-done | bytes 4194320 | tf_op jit(solution)/shard_map/all_gather | solution.py:228
  147.9 2.2 copy-done.1
  150.1 11.7 %placed_update.2.refs_0_ = f32[2,128,1024]{2,1,0:T(8,128)S(1)} custom-call(s32[2]{0:T(128)S(1)} %get-tuple-element.34.index_ref, s32[2]{0:T(128)S(1)} %get-tuple-element.31.valid_ref, f32[1024,1024]{1,0:T(8,128)S(1)} %bitcast.53, f32[1024,1024]{1,0:T(8,128)} %bitcast.63), custom_call_target="tpu_custom_call" | custom-call | flops 3221225472 | bytes 8388608 | tf_op jit(solution)/shard_map/placed_update/pallas_call | solution.py:186
  161.8 1.3 collective-permute-start.5
  163.1 1.3 collective-permute-start.4
  164.4 1.3 collective-permute-start.3
  165.7 2.5 slice_bitcast_fusion
  168.2 0.8 fusion.4
  173.0 0.1 add_convert_fusion.flags_ref
  173.0 1.3 collective-permute-start
  174.4 29.0 %collective-permute-done = f32[8]{0:T(128)S(1)} collective-permute-done((f32[8]{0:T(128)S(1)}, f32[8]{0:T(128)S(1)}, u32[]{:S(2)}, u32[]{:S(2)}) %collective-permute-start) | collective-permute-done | bytes 64 | tf_op jit(solution)/shard_map/ppermute | solution.py:21
  203.4 9.7 %collective-permute-done.4.refs_2_ = f32[2,128,1024]{2,1,0:T(8,128)S(1)} collective-permute-done((f32[2,128,1024]{2,1,0:T(8,128)S(1)}, f32[2,128,1024]{2,1,0:T(8,128)S(1)}, u32[]{:S(2)}, u32[]{:S(2)}) %collective-permute-start.4) | collective-permute-done | bytes 1048608 | tf_op jit(solution)/shard_map/ppermute | solution.py:21
  213.1 4.4 %assemble.2 = f32[2,128,2048]{2,1,0:T(8,128)} custom-call(s32[4,8]{1,0:T(4,128)S(1)} %pad_add_fusion.places_ref, s32[4]{0:T(128)S(1)} %add_convert_fusion.flags_ref, f32[2,128,2048]{2,1,0:T(8,128)} %get-tuple-element.26.base_ref, f32[2,128,1024]{2,1,0:T(8,128)S(1)} %placed_update.2.refs_0_, f32[2,128,1024]{2,1,0:T(8,128)} %collective-permute-done.3.refs_1_, ...), custom_call_target="tpu_custom_call" | custom-call | flops 524288 | bytes 8388608 | tf_op jit(solution)/shard_map/assemble/pallas_call | solution.py:216
  217.5 2.3 slice.69
  219.8 0.0 all-gather.11.cloned.1.call-start
  219.9 2.2 copy-done.2
  222.1 2.3 placed_update.3.refs_0_
  224.3 1.3 collective-permute-start.8
  225.6 1.3 collective-permute-start.7
  226.9 1.5 collective-permute-start.6
  228.4 62.0 %all-gather.17.cloned.1.call-done = f32[2,512,1024]{2,1,0:T(8,128)} async-done(((f32[2,128,1024]{2,1,0:T(8,128)}), f32[2,512,1024]{2,1,0:T(8,128)}) %all-gather.17.cloned.1.call-update) | async-done | bytes 4194320 | tf_op jit(solution)/shard_map/all_gather | solution.py:228
  290.4 50.1 %factor_columns.3 = (f32[1024,1024]{1,0:T(8,128)S(1)}, f32[1024,128]{1,0:T(8,128)S(1)}) custom-call(f32[1024,1024]{1,0:T(8,128)} %bitcast.65), custom_call_target="tpu_custom_call" | custom-call | flops 99999997952 | bytes 8388608 | tf_op jit(solution)/shard_map/factor_columns/pallas_call | solution.py:121
  340.6 2.0 copy-done
  342.6 4.4 %assemble.3 = f32[2,128,2048]{2,1,0:T(8,128)} custom-call(s32[4,8]{1,0:T(4,128)S(1)} %pad_add_fusion.places_ref, s32[4]{0:T(128)S(1)} %add_convert_fusion.flags_ref, f32[2,128,2048]{2,1,0:T(8,128)} %get-tuple-element.25.base_ref, f32[2,128,1024]{2,1,0:T(8,128)S(1)} %placed_update.3.refs_0_, f32[2,128,1024]{2,1,0:T(8,128)} %collective-permute-done.6.refs_1_, ...), custom_call_target="tpu_custom_call" | custom-call | flops 524288 | bytes 8388608 | tf_op jit(solution)/shard_map/assemble/pallas_call | solution.py:216
  347.0 1.3 slice.71
  348.3 10.2 %solve_low.1 = f32[256,1024]{1,0:T(8,128)} custom-call(f32[1024,1024]{1,0:T(8,128)} %copy-done, f32[1024,128]{1,0:T(8,128)S(1)} %get-tuple-element.8.refs_4_.inverses_ref, f32[256,1024]{1,0:T(8,128)S(1)} %bitcast.51), custom_call_target="tpu_custom_call" | custom-call | flops 1610612736 | bytes 4194304 | tf_op jit(solution)/shard_map/solve_low/pallas_call | solution.py:149
  359.9 2.6 slice.51
  362.4 0.1 dynamic-slice_bitcast_fusion.1
  362.5 1.5 maximum_bitcast_fusion
  364.0 1.3 dynamic-slice_bitcast_fusion
  365.3 2.8 maximum_select_fusion
  368.1 37.2 %all-gather.11.cloned.1.call-done = f32[2,4,128,1024]{3,2,0,1:T(8,128)} async-done(((f32[2,1,128,1024]{3,2,0,1:T(8,128)}), f32[2,4,128,1024]{3,2,0,1:T(8,128)}) %all-gather.11.cloned.1.call-update) | async-done | bytes 4194320 | tf_op jit(solution)/shard_map/all_gather | solution.py:228
  405.3 2.5 copy.23
  407.8 5.9 %fusion.1 = f32[1,2,1,128,1024]{4,3,2,1,0:T(8,128)} fusion(f32[2,128,2048]{2,1,0:T(8,128)S(1)} %copy-done.5, pred[]{:T(512)S(6)} %or.3, f32[2,128,1024]{2,1,0:T(8,128)} %bitcast.28, f32[1024,1024,1]{1,0,2:T(8,128)S(1)} %bitcast.56), kind=kOutput, calls=%fused_computation.6 | convolution fusion | flops 3221749760 | bytes 7340033 | tf_op jit(solution)/shard_map/dot_general | solution.py:25
  (32 shorter events, 0.1 us)
Async XLA Ops:
  7.2 40.9 %all-gather.13.cloned.1.call-start = ((), (), s32[]{:S(2)}) async-start(), calls=%async_computation.2 | async-start | bytes 5242880 | tf_op jit(solution)/shard_map/all_gather | solution.py:228
  10.8 105.5 %all-gather.15.cloned.1.call-start = ((), (), s32[]{:S(2)}) async-start(), calls=%async_computation.3 | async-start | bytes 5242880 | tf_op jit(solution)/shard_map/all_gather | solution.py:228
  11.5 136.4 %all-gather.9.cloned.1.call-start = ((), (), s32[]{:S(2)}) async-start(), calls=%async_computation | async-start | bytes 5242880 | tf_op jit(solution)/shard_map/all_gather | solution.py:228
  48.1 2.2 copy-start.3
  50.3 63.0 %copy-start.7 = (s32[1,8]{1,0:T(1,128)S(1)}, s32[1,8]{1,0:T(1,128)}, u32[]{:S(2)}) copy-start(s32[1,8]{1,0:T(1,128)} %param.7) | copy-start | bytes 100
  113.3 177.2 %all-gather.17.cloned.1.call-start = ((), (), s32[]{:S(2)}) async-start(), calls=%async_computation.4 | async-start | bytes 5242880 | tf_op jit(solution)/shard_map/all_gather | solution.py:228
  113.3 59.7 %collective-permute-start.2 = (f32[8]{0:T(128)S(1)}, f32[8]{0:T(128)S(1)}, u32[]{:S(2)}, u32[]{:S(2)}) collective-permute-start(f32[8]{0:T(128)S(1)} %bitcast_convert_fusion), channel_id=1, source_target_pairs={{12,0},{16,4},{20,8},{24,12},{28,16},{13,1},{17,5},{21,9},{25,13},... | collective-permute-start | bytes 104 | tf_op jit(solution)/shard_map/ppermute | solution.py:21
  114.6 59.7 %collective-permute-start.1 = (f32[8]{0:T(128)S(1)}, f32[8]{0:T(128)S(1)}, u32[]{:S(2)}, u32[]{:S(2)}) collective-permute-start(f32[8]{0:T(128)S(1)} %bitcast_convert_fusion), channel_id=1, source_target_pairs={{8,0},{12,4},{16,8},{20,12},{24,16},{28,20},{9,1},{13,5},{17,9},{2... | collective-permute-start | bytes 104 | tf_op jit(solution)/shard_map/ppermute | solution.py:21
  147.9 2.2 copy-start.1
  150.1 15.6 %copy-start.6 = (f32[1,4,1,128,2048]{4,3,2,1,0:T(8,128)S(1)}, f32[1,4,1,128,2048]{4,3,2,1,0:T(8,128)}, u32[]{:S(2)}) copy-start(f32[1,4,1,128,2048]{4,3,2,1,0:T(8,128)} %param.5) | copy-start | bytes 12582916
  161.8 41.6 %collective-permute-start.5 = (f32[2,128,1024]{2,1,0:T(8,128)S(1)}, f32[2,128,1024]{2,1,0:T(8,128)S(1)}, u32[]{:S(2)}, u32[]{:S(2)}) collective-permute-start(f32[2,128,1024]{2,1,0:T(8,128)S(1)} %placed_update.2.refs_0_), channel_id=1, source_target_pairs={{12,0},{16,4},{20,8},{24,12},{28,16},{13,1},{17,5},{21,9},{25,13},... | collective-permute-start | bytes 3145736 | tf_op jit(solution)/shard_map/ppermute | solution.py:21
  163.1 50.1 %collective-permute-start.4 = (f32[2,128,1024]{2,1,0:T(8,128)S(1)}, f32[2,128,1024]{2,1,0:T(8,128)S(1)}, u32[]{:S(2)}, u32[]{:S(2)}) collective-permute-start(f32[2,128,1024]{2,1,0:T(8,128)S(1)} %placed_update.2.refs_0_), channel_id=1, source_target_pairs={{8,0},{12,4},{16,8},{20,12},{24,16},{28,20},{9,1},{13,5},{17,9},{2... | collective-permute-start | bytes 3145736 | tf_op jit(solution)/shard_map/ppermute | solution.py:21
  164.4 48.8 %collective-permute-start.3 = (f32[2,128,1024]{2,1,0:T(8,128)S(1)}, f32[2,128,1024]{2,1,0:T(8,128)}, u32[]{:S(2)}, u32[]{:S(2)}) collective-permute-start(f32[2,128,1024]{2,1,0:T(8,128)S(1)} %placed_update.2.refs_0_), channel_id=1, source_target_pairs={{4,0},{8,4},{12,8},{16,12},{20,16},{24,20},{28,24},{5,1},{9,5},{13... | collective-permute-start | bytes 3145736 | tf_op jit(solution)/shard_map/ppermute | solution.py:21
  165.7 2.5 copy-start.8
  173.0 30.3 %collective-permute-start = (f32[8]{0:T(128)S(1)}, f32[8]{0:T(128)S(1)}, u32[]{:S(2)}, u32[]{:S(2)}) collective-permute-start(f32[8]{0:T(128)S(1)} %bitcast_convert_fusion), channel_id=1, source_target_pairs={{4,0},{8,4},{12,8},{16,12},{20,16},{24,20},{28,24},{5,1},{9,5},{13... | collective-permute-start | bytes 104 | tf_op jit(solution)/shard_map/ppermute | solution.py:21
  219.8 185.4 %all-gather.11.cloned.1.call-start = ((), (), s32[]{:S(2)}) async-start(), calls=%async_computation.1 | async-start | bytes 5242880 | tf_op jit(solution)/shard_map/all_gather | solution.py:228
  219.9 2.2 copy-start.2
  224.3 118.3 %collective-permute-start.8 = (f32[2,128,1024]{2,1,0:T(8,128)S(1)}, f32[2,128,1024]{2,1,0:T(8,128)S(1)}, u32[]{:S(2)}, u32[]{:S(2)}) collective-permute-start(f32[2,128,1024]{2,1,0:T(8,128)S(1)} %placed_update.3.refs_0_), channel_id=1, source_target_pairs={{12,0},{16,4},{20,8},{24,12},{28,16},{13,1},{17,5},{21,9},{25,13},... | collective-permute-start | bytes 3145736 | tf_op jit(solution)/shard_map/ppermute | solution.py:21
  225.6 117.0 %collective-permute-start.7 = (f32[2,128,1024]{2,1,0:T(8,128)S(1)}, f32[2,128,1024]{2,1,0:T(8,128)S(1)}, u32[]{:S(2)}, u32[]{:S(2)}) collective-permute-start(f32[2,128,1024]{2,1,0:T(8,128)S(1)} %placed_update.3.refs_0_), channel_id=1, source_target_pairs={{8,0},{12,4},{16,8},{20,12},{24,16},{28,20},{9,1},{13,5},{17,9},{2... | collective-permute-start | bytes 3145736 | tf_op jit(solution)/shard_map/ppermute | solution.py:21
  226.9 115.7 %collective-permute-start.6 = (f32[2,128,1024]{2,1,0:T(8,128)S(1)}, f32[2,128,1024]{2,1,0:T(8,128)}, u32[]{:S(2)}, u32[]{:S(2)}) collective-permute-start(f32[2,128,1024]{2,1,0:T(8,128)S(1)} %placed_update.3.refs_0_), channel_id=1, source_target_pairs={{4,0},{8,4},{12,8},{16,12},{20,16},{24,20},{28,24},{5,1},{9,5},{13... | collective-permute-start | bytes 3145736 | tf_op jit(solution)/shard_map/ppermute | solution.py:21
  340.6 2.0 copy-start
  359.8 2.7 copy-start.4
  368.1 39.7 %copy-start.5 = (f32[2,128,2048]{2,1,0:T(8,128)S(1)}, f32[2,128,2048]{2,1,0:T(8,128)}, u32[]{:S(2)}) copy-start(f32[2,128,2048]{2,1,0:T(8,128)} %assemble.3) | copy-start | bytes 6291460
Sparse Core Ops, SparseCore 0:
  10.9 37.1 all-gather.12
  50.2 34.6 all-gather.14
  113.4 34.4 all-gather.8
  219.9 70.4 all-gather.16
  358.7 46.5 all-gather.10
